TPU v7x, 512 devices: a whole 4x8x8 slice. The times are simulated.
512 devices in a mesh: module: 4 (over y_lo), dp: 128 (over x, y_hi, z, core).
Axes of the slice: x: 4, y: 8 (y_hi: 2, y_lo: 4; y = y_hi * 4 + y_lo), z: 8, core: 2. Of those that a mesh axis runs over, the one named last changes fastest.
Arguments:
- weight: bfloat16 [4, 1024, 1024], P('module'), may hold values from -0.1875 to 0.1875
- replay_buffer: bfloat16 [4, 2, 16384, 1024], P('module', None, 'dp'), may hold values from -6 to 6
- slot_index: int32 [4, 2], P('module'), may hold values from 0 to 1
- stem_input: bfloat16 [2, 16384, 1024], P(None, 'dp'), may hold values from -6 to 6
- top_grad: bfloat16 [2, 16384, 1024], P(None, 'dp'), may hold values from -6 to 6
- late_grad: bfloat16 [4, 16384, 1024], P('module', 'dp'), may hold values from -6 to 6
Outputs:
- weight_grad: bfloat16 [4, 1024, 1024], P('module')
- handoff: bfloat16 [4, 16384, 1024], P('module', 'dp')
- returned_grad: bfloat16 [4, 16384, 1024], P('module', 'dp')
All inputs are finite; a program needn't handle non-finite values.
Results may differ from a plain program's by a relative error of at most 0.007.
Values may be sent and summed in bfloat16 or wider, within the bound.
No kernel may reach another device: no remote copies, remote signals or barrier semaphores. Data moves between devices by JAX's collectives and lax.ppermute only.
A program may use at most 64 MiB of HBM per device.

v0:
```python
import jax
import jax.numpy as jnp
from jax import lax
from jax.sharding import PartitionSpec as P


def from_behind(block, axis, distance):
    devices = range(lax.axis_size(axis))
    route = [(i - distance, i) for i in devices if i - distance in devices]
    return lax.ppermute(block, axis, route)


def normalize(rows):
    values = rows.astype(jnp.float32)
    centered = values - jnp.mean(values, axis=-1, keepdims=True)
    inverse = lax.rsqrt(jnp.mean(centered * centered, axis=-1, keepdims=True) + 1e-06)
    return (centered * inverse, inverse)


def forward(rows, matrix):
    normed, inverse = normalize(rows)
    preact = jnp.dot(normed.astype(jnp.bfloat16), matrix, preferred_element_type=jnp.float32)
    return (rows.astype(jnp.float32) + jax.nn.gelu(preact)).astype(jnp.bfloat16)


def backward(rows, matrix, upstream):
    normed, inverse = normalize(rows)
    rounded = normed.astype(jnp.bfloat16)
    preact = jnp.dot(rounded, matrix, preferred_element_type=jnp.float32)
    unused, pullback = jax.vjp(jax.nn.gelu, preact)
    pre_grad = pullback(upstream.astype(jnp.float32))[0].astype(jnp.bfloat16)
    weight_part = lax.dot_general(
        rounded, pre_grad, (((0,), (0,)), ((), ())), preferred_element_type=jnp.float32
    )
    norm_grad = lax.dot_general(
        pre_grad, matrix, (((1,), (1,)), ((), ())), preferred_element_type=jnp.float32
    )
    centred_grad = norm_grad - jnp.mean(norm_grad, axis=-1, keepdims=True)
    centred_grad = centred_grad - normed * jnp.mean(norm_grad * normed, axis=-1, keepdims=True)
    input_grad = upstream.astype(jnp.float32) + inverse * centred_grad
    return (input_grad.astype(jnp.bfloat16), weight_part)


def per_device(weight, replay_buffer, slot_index, stem_input, top_grad, late_grad):
    matrix = weight[0]
    stored = replay_buffer[0]
    slot_rows = slot_index[0]
    module_number = lax.axis_index("module")
    module_count = lax.axis_size("module")
    is_first = module_number == 0
    is_last = module_number == module_count - 1
    returning = late_grad[0]
    step_count = stem_input.shape[0]
    summed = jnp.zeros(matrix.shape, jnp.float32)
    arriving = lax.dynamic_index_in_dim(stored, slot_rows[0], 0, keepdims=False)
    fresh_out = arriving
    sent_back = returning
    for step_number in range(step_count):
        replayed = lax.dynamic_index_in_dim(stored, slot_rows[step_number], 0, keepdims=False)
        fresh_in = jnp.where(is_first, stem_input[step_number], arriving)
        fresh_out = forward(fresh_in, matrix)
        delayed = jnp.where(is_last, top_grad[step_number], returning)
        sent_back, weight_part = backward(replayed, matrix, delayed)
        summed = summed + weight_part
        if step_number + 1 < step_count:
            arriving = from_behind(fresh_out, "module", 1)
            returning = from_behind(sent_back, "module", -1)
    grad_scale = float(step_count * stem_input.shape[1] * lax.axis_size("dp")) ** (-0.5)
    weight_grad = (lax.psum(summed, "dp") * grad_scale).astype(jnp.bfloat16)
    return (weight_grad[None], fresh_out[None], sent_back[None])


def solution(mesh):
    placed = (
        P("module", None, None),
        P("module", None, "dp", None),
        P("module", None),
        P(None, "dp", None),
        P(None, "dp", None),
        P("module", "dp", None),
    )
    return jax.shard_map(
        per_device,
        mesh=mesh,
        in_specs=placed,
        out_specs=(P("module", None, None), P("module", "dp", None), P("module", "dp", None)),
        check_vma=False,
    )
```

profile of v0, /device:TPU:1, one launch (start us, length us, event | category | flops | bytes accessed | tf_op | source)
XLA Modules:
  0.0 1615.5 jit_solution(8505914132753083932)
XLA Ops:
  7.2 0.0 copy-start
  7.2 0.0 all-reduce.2.cloned.1.call-start
  7.2 1.4 fusion.131
  11.9 1.1 convert_reduce_fusion.2
  13.6 1.1 convert_reduce_fusion.3
  14.7 1.2 fusion.25
  15.9 1.9 fusion.32
  17.9 1.0 fusion.130
  18.8 0.0 copy-done.3
  18.9 0.1 copy-done.5
  19.0 0.3 fusion.88
  19.2 1.3 collective-permute-start
  20.5 0.8 fusion.102
  21.4 5.6 collective-permute-done
  27.0 0.7 copy-done.6
  27.7 0.8 fusion.39
  28.5 2.8 convolution_add_fusion
  31.3 0.0 all-reduce.2.cloned.1.call-update
  31.4 0.9 fusion.129
  32.3 0.1 copy-done.2
  32.4 0.2 copy-done.4
  32.5 0.1 copy-done.7
  32.6 1.0 convert_reduce_fusion.1
  33.6 0.2 fusion.57
  33.8 0.6 fusion.58
  34.5 5.3 collective-permute-start.1
  39.8 3.3 collective-permute-done.1
  43.1 0.2 convert_reduce_fusion
  43.2 0.2 fusion.20
  43.5 1.3 fusion.82
  44.8 1559.7 %all-reduce.2.cloned.1.call-done = f32[1024,1024]{1,0:T(8,128)} async-done(((f32[1024,1024]{1,0:T(8,128)}), f32[1024,1024]{1,0:T(8,128)}) %all-reduce.2.cloned.1.call-update) | async-done | bytes 4194320 | tf_op jit(solution)/shard_map/psum | solution.py:69
  1604.5 4.1 fusion
  (20 shorter events, 0.1 us)
Async XLA Ops:
  7.2 8.7 copy-start
  7.2 1597.4 %all-reduce.2.cloned.1.call-start = ((), (), s32[]{:S(2)}) async-start(), calls=%async_computation | async-start | bytes 8388608 | tf_op jit(solution)/shard_map/psum | solution.py:69
  15.9 2.0 copy-start.1
  17.8 1.0 copy-start.3
  17.9 1.1 copy-start.5
  19.2 7.8 collective-permute-start
  27.0 0.7 copy-start.6
  31.3 1.0 copy-start.2
  31.3 1.2 copy-start.4
  31.4 1.2 copy-start.7
  34.5 8.6 collective-permute-start.1
Sparse Core Ops, SparseCore 0:
  31.4 1573.0 all-reduce.1
where the time goes:
time: 1620 us
  waiting for transfers between devices  1570 us (97%)
  between operations  18.1 us (1%)
    psum x1, waiting for transfers between devices, per_device(): weight_grad = (lax.psum(summed, 'dp') * grad_scale).astype(jnp.bfloat16)  1560 us
  transfers between devices with their start and end apart: 3, of which 3 were waited for; matrix products, arithmetic and copies ran while one was open for 0% of the time, Pallas kernels for 0%

commit v1 on v0

--- a/solution.py
+++ b/solution.py
@@ -1,7 +1,7 @@
 import jax
 import jax.numpy as jnp
 from jax import lax
-from jax.sharding import PartitionSpec as P
+from jax.sharding import Mesh, PartitionSpec as P
 
 
 def from_behind(block, axis, distance):
@@ -41,6 +41,30 @@
     return (input_grad.astype(jnp.bfloat16), weight_part)
 
 
+DP = ("x", "y_hi", "z", "core")
+PLANE = ("x", "z")
+
+
+def exchange(block, axes):
+    return lax.all_to_all(block, axes, 0, 0, tiled=True)
+
+
+def replica_sum(part, scale):
+    rows, columns = part.shape
+    cores, plane, halves = (lax.axis_size(axes) for axes in ("core", PLANE, "y_hi"))
+    pair = exchange(part.astype(jnp.bfloat16), "core").reshape(cores, rows // cores, columns)
+    chip = jnp.sum(pair.astype(jnp.float32), axis=0).astype(jnp.bfloat16)
+    piece = rows // cores // plane
+    spread = exchange(chip, PLANE).reshape(plane, piece, columns)
+    own = jnp.sum(spread.astype(jnp.float32), axis=0)
+    other = lax.ppermute(own, "y_hi", [(i, (i + 1) % halves) for i in range(halves)])
+    total = ((own + other) * scale).astype(jnp.bfloat16)
+    sent = jnp.broadcast_to(total[None], (plane, piece, columns)).reshape(plane * piece, columns)
+    half = exchange(sent, PLANE)
+    sent = jnp.broadcast_to(half[None], (cores, rows // cores, columns)).reshape(rows, columns)
+    return exchange(sent, "core")
+
+
 def per_device(weight, replay_buffer, slot_index, stem_input, top_grad, late_grad):
     matrix = weight[0]
     stored = replay_buffer[0]
@@ -65,24 +89,29 @@
         if step_number + 1 < step_count:
             arriving = from_behind(fresh_out, "module", 1)
             returning = from_behind(sent_back, "module", -1)
-    grad_scale = float(step_count * stem_input.shape[1] * lax.axis_size("dp")) ** (-0.5)
-    weight_grad = (lax.psum(summed, "dp") * grad_scale).astype(jnp.bfloat16)
+    replicas = lax.axis_size(DP)
+    grad_scale = float(step_count * stem_input.shape[1] * replicas) ** (-0.5)
+    weight_grad = replica_sum(summed, grad_scale)
     return (weight_grad[None], fresh_out[None], sent_back[None])
 
 
 def solution(mesh):
+    modules, replicas = (mesh.shape[name] for name in ("module", "dp"))
+    fine = Mesh(
+        mesh.devices.reshape(modules, 4, 2, replicas // 16, 2), ("module", *DP)
+    )
     placed = (
         P("module", None, None),
-        P("module", None, "dp", None),
+        P("module", None, DP, None),
         P("module", None),
-        P(None, "dp", None),
-        P(None, "dp", None),
-        P("module", "dp", None),
+        P(None, DP, None),
+        P(None, DP, None),
+        P("module", DP, None),
     )
     return jax.shard_map(
         per_device,
-        mesh=mesh,
+        mesh=fine,
         in_specs=placed,
-        out_specs=(P("module", None, None), P("module", "dp", None), P("module", "dp", None)),
+        out_specs=(P("module", None, None), P("module", DP, None), P("module", DP, None)),
         check_vma=False,
     )

time: 1620 us -> 133 us (0.08)
  waiting for transfers between devices: 1570 us -> 46.8 us
  starting transfers between devices: 6.64 us -> 30.8 us
  blocking collectives: 0 us -> 23.7 us
    psum x1 -> x0, waiting for transfers between devices: 1560 us -> none  [per_device(): weight_grad = (lax.psum(summed, 'dp') * grad_scale).astype(jnp.bfloat16)]
    all_to_all x0 -> x2, waiting for transfers between devices: none -> 36.9 us  [exchange(): return lax.all_to_all(block, axes, 0, 0, tiled=True)]
    all_to_all x0 -> x2, blocking collectives: none -> 23.7 us  [exchange(): return lax.all_to_all(block, axes, 0, 0, tiled=True)]
    all_to_all x0 -> x2, starting transfers between devices: none -> 17.4 us  [exchange(): return lax.all_to_all(block, axes, 0, 0, tiled=True)]
  transfers between devices with their start and end apart: 3 -> 5, of which waited for: 3 -> 4; matrix products, arithmetic and copies ran while one was open for 0% -> 5% of each run, Pallas kernels for 0% -> 0%
where the time goes in v1:
time: 133 us; the launch traced here: 131 us
  waiting for transfers between devices  46.8 us (35%)
  starting transfers between devices  30.8 us (23%)
  blocking collectives  23.7 us (18%)
  other arithmetic  11.1 us (8%)
  matrix products  8.25 us (6%)
  local copies, waits for them, and re-layouts  6.13 us (5%)
  between operations  4.73 us (4%)
    all_to_all x2, waiting for transfers between devices, exchange(): return lax.all_to_all(block, axes, 0, 0, tiled=True)  36.9 us
    all_to_all x2, blocking collectives, exchange(): return lax.all_to_all(block, axes, 0, 0, tiled=True)  23.7 us
    all_to_all x2, starting transfers between devices, exchange(): return lax.all_to_all(block, axes, 0, 0, tiled=True)  17.4 us
    ppermute x2, waiting for transfers between devices, from_behind(): return lax.ppermute(block, axis, route)  9.96 us
    ppermute x1, starting transfers between devices, replica_sum(): lax.ppermute(own, 'y_hi', [(i, (i + 1) % halves) for i in range(halves)])  7.44 us
    ppermute x2, starting transfers between devices, from_behind(): return lax.ppermute(block, axis, route)  5.98 us
    reduce_sum x4, other arithmetic, normalize(): centered = values - jnp.mean(values, axis=-1, keepdims=True)  4.4 us
    reduce_sum x1, other arithmetic, replica_sum(): chip = jnp.sum(pair.astype(jnp.float32), axis=0).astype(jnp.bfloat16)  3.32 us
  transfers between devices with their start and end apart: 5, of which 4 were waited for; matrix products, arithmetic and copies ran while one was open for 5% of the time, Pallas kernels for 0%

profile of v1, /device:TPU:1, one launch (start us, length us, event | category | flops | bytes accessed | tf_op | source)
XLA Modules:
  0.0 131.5 jit_solution(15962197337004013037)
XLA Ops:
  0.6 1.4 %fusion.130 = (s32[1,1]{1,0:T(1,128)}, s32[1,1]{1,0:T(1,128)}) fusion(s32[1,2]{1,0:T(1,128)} %param.8), kind=kLoop, calls=%fused_computation.155 | loop fusion | bytes 16 | tf_op jit(solution)/shard_map/slice | solution.py:83
  5.3 1.1 convert_reduce_fusion.4
  6.4 1.2 fusion.24
  8.2 1.1 convert_reduce_fusion.3
  9.3 1.9 %fusion.31 = bf16[128,1024]{1,0:T(8,128)(2,1)S(1)} fusion(bf16[1,1024,1024]{2,1,0:T(8,128)(2,1)S(1)} %copy-done, f32[128]{0:T(128)S(1)} %add_rsqrt_fusion.3, f32[128]{0:T(128)S(1)} %broadcast_multiply_fusion.7, bf16[1,128,1024]{2,1,0:T(8,128)(2,1)} %param.11, bf16[2,128,1024]{2,1,0:T(8,128)(2,1)} %param.10, pred[]{:T(512)S(6)} %eq.6, ...), kind=kOutput, calls=%fused_computation.56 | convolution fusion | flops 271843328 | bytes 3146757 | tf_op jit(solution)/shard_map/dot_general | solution.py:29
  11.3 1.0 fusion.129
  12.4 0.3 fusion.87
  12.7 1.3 collective-permute-start
  14.0 0.8 fusion.101
  14.8 5.6 %collective-permute-done = bf16[128,1024]{1,0:T(8,128)(2,1)S(1)} collective-permute-done((bf16[128,1024]{1,0:T(8,128)(2,1)S(1)}, bf16[128,1024]{1,0:T(8,128)(2,1)S(1)}, u32[]{:S(2)}, u32[]{:S(2)}) %collective-permute-start) | collective-permute-done | bytes 262176 | tf_op jit(solution)/shard_map/ppermute | solution.py:10
  20.4 0.7 copy-done.5
  21.1 0.8 fusion.38
  21.9 0.8 add_convert_fusion
  22.8 13.3 %all_to_all.30 = bf16[2,512,1024]{2,1,0:T(8,128)(2,1)} all-to-all(bf16[2,512,1024]{2,1,0:T(8,128)(2,1)S(1)} %bitcast.116), channel_id=1, replica_groups=mesh['module'=4,'x'=4,'y_hi'=2,'z'=8,'core'=2] {'core'}, dimensions={0} | all-to-all | bytes 4194304 | tf_op jit(solution)/shard_map/all_to_all | solution.py:49
  36.1 3.3 %reduce_sum.135 = bf16[512,1024]{1,0:T(8,128)(2,1)} reduce(bf16[2,512,1024]{2,1,0:T(8,128)(2,1)} %all_to_all.30, bf16[]{:T(256)} %constant.54.clone.1), dimensions={0}, to_apply=%region_6.7 | reduce | flops 524288 | bytes 3145730 | tf_op jit(solution)/shard_map/reduce_sum | solution.py:56
  39.4 9.3 %all-to-all-start.1 = ((bf16[32,16,1024]{2,1,0:T(8,128)(2,1)}), bf16[32,16,1024]{2,1,0:T(8,128)(2,1)}, u32[]{:S(2)}, u32[]{:S(2)}) async-start(bf16[32,16,1024]{2,1,0:T(8,128)(2,1)} %bitcast.117), calls=%async_computation.1 | async-start | bytes 2097152 | tf_op jit(solution)/shard_map/all_to_all | solution.py:49
  48.7 0.9 fusion.128
  49.7 24.2 %all-to-all-done.1 = bf16[32,16,1024]{2,1,0:T(8,128)(2,1)} async-done(((bf16[32,16,1024]{2,1,0:T(8,128)(2,1)}), bf16[32,16,1024]{2,1,0:T(8,128)(2,1)}, u32[]{:S(2)}, u32[]{:S(2)}) %all-to-all-start.1) | async-done | bytes 1048608 | tf_op jit(solution)/shard_map/all_to_all | solution.py:49
  73.9 1.4 %convert_reduce_fusion = f32[16,1024]{1,0:T(8,128)S(1)} fusion(bf16[32,16,1024]{2,1,0:T(8,128)(2,1)} %all-to-all-done.1), kind=kLoop, calls=%fused_computation.13 | loop fusion | flops 1032192 | bytes 1114112 | tf_op jit(solution)/shard_map/reduce_sum | solution.py:59
  75.3 7.4 %collective-permute-start.1 = (f32[16,1024]{1,0:T(8,128)S(1)}, f32[16,1024]{1,0:T(8,128)S(1)}, u32[]{:S(2)}, u32[]{:S(2)}) collective-permute-start(f32[16,1024]{1,0:T(8,128)S(1)} %convert_reduce_fusion), channel_id=1, source_target_pairs={{0,16},{16,0},{1,17},{17,1},{2,18},{18,2},{3,19},{19,3},{4,20},{20... | collective-permute-start | bytes 196616 | tf_op jit(solution)/shard_map/ppermute | solution.py:60
  82.7 2.1 %convert_reduce_fusion.2 = (f32[128]{0:T(128)S(1)}, bf16[128,1024]{1,0:T(8,128)(2,1)S(1)}, bf16[1,128,1024]{2,1,0:T(8,128)(2,1)}) fusion(bf16[1,2,128,1024]{3,2,1,0:T(8,128)(2,1)S(1)} %copy-done.1, s32[]{:T(128)S(6)} %select_n.38, bf16[2,128,1024]{2,1,0:T(8,128)(2,1)} %param.9, pred[]{:T(512)S(6)} %eq.7, f32[128]{0:T(128)S(1)} %broadcast_multiply_fusion, ...), kind=kLoop, calls=%fused_computation.24 | loop fusion | flops 1834880 | bytes 2361866 | tf_op jit(solution)/shard_map/reduce_sum | solution.py:15
  84.9 1.1 broadcast_in_dim.12
  85.9 8.1 %all-to-all-start.2 = ((bf16[32,16,1024]{2,1,0:T(8,128)(2,1)}), bf16[32,16,1024]{2,1,0:T(8,128)(2,1)}, u32[]{:S(2)}, u32[]{:S(2)}) async-start(bf16[32,16,1024]{2,1,0:T(8,128)(2,1)} %broadcast_in_dim.12), calls=%async_computation.2 | async-start | bytes 2097152 | tf_op jit(solution)/shard_map/all_to_all | solution.py:49
  94.3 0.6 fusion.57
  94.9 4.7 %collective-permute-start.2 = (bf16[128,1024]{1,0:T(8,128)(2,1)S(1)}, bf16[128,1024]{1,0:T(8,128)(2,1)S(1)}, u32[]{:S(2)}, u32[]{:S(2)}) collective-permute-start(bf16[128,1024]{1,0:T(8,128)(2,1)S(1)} %fusion.57), channel_id=1, source_target_pairs={{0,128},{128,256},{256,384},{1,129},{129,257},{257,385},{2,130},{1... | collective-permute-start | bytes 786440 | tf_op jit(solution)/shard_map/ppermute | solution.py:10
  99.6 4.3 %collective-permute-done.2 = bf16[128,1024]{1,0:T(8,128)(2,1)S(1)} collective-permute-done((bf16[128,1024]{1,0:T(8,128)(2,1)S(1)}, bf16[128,1024]{1,0:T(8,128)(2,1)S(1)}, u32[]{:S(2)}, u32[]{:S(2)}) %collective-permute-start.2) | collective-permute-done | bytes 262176 | tf_op jit(solution)/shard_map/ppermute | solution.py:10
  104.1 0.2 fusion.19
  104.3 1.3 %fusion.81 = bf16[1,128,1024]{2,1,0:T(8,128)(2,1)} fusion(bf16[1,1024,1024]{2,1,0:T(8,128)(2,1)S(1)} %copy-done, bf16[128,1024]{1,0:T(8,128)(2,1)S(1)} %get-tuple-element.9, f32[128]{0:T(128)S(1)} %add_rsqrt_fusion, f32[128]{0:T(128)S(1)} %broadcast_multiply_fusion.2), kind=kOutput, calls=%fused_computation.98 | convolution fusion | flops 270401536 | bytes 2622464 | tf_op jit(solution)/shard_map/dot_general | solution.py:22
  105.7 12.6 %all-to-all-done.2 = bf16[32,16,1024]{2,1,0:T(8,128)(2,1)} async-done(((bf16[32,16,1024]{2,1,0:T(8,128)(2,1)}), bf16[32,16,1024]{2,1,0:T(8,128)(2,1)}, u32[]{:S(2)}, u32[]{:S(2)}) %all-to-all-start.2) | async-done | bytes 1048608 | tf_op jit(solution)/shard_map/all_to_all | solution.py:49
  118.3 1.5 %broadcast_in_dim.14 = bf16[2,512,1024]{2,1,0:T(8,128)(2,1)S(1)} broadcast(bf16[512,1024]{1,0:T(8,128)(2,1)} %bitcast.12), dimensions={1,2} | broadcast | bytes 3145728 | tf_op jit(solution)/shard_map/broadcast_in_dim | solution.py:64
  119.8 10.4 %all_to_all.31 = bf16[2,512,1024]{2,1,0:T(8,128)(2,1)S(1)} all-to-all(bf16[2,512,1024]{2,1,0:T(8,128)(2,1)S(1)} %broadcast_in_dim.14), channel_id=1, replica_groups=mesh['module'=4,'x'=4,'y_hi'=2,'z'=8,'core'=2] {'core'}, dimensions={0} | all-to-all | bytes 4194304 | tf_op jit(solution)/shard_map/all_to_all | solution.py:49
  130.2 1.3 %copy.10 = bf16[1,1024,1024]{2,1,0:T(8,128)(2,1)} copy(bf16[1,1024,1024]{2,1,0:T(8,128)(2,1)S(1)} %bitcast.115) | data formatting | bytes 4194304
  (26 shorter events, 0.6 us)
Async XLA Ops:
  0.6 8.7 %copy-start = (bf16[1,1024,1024]{2,1,0:T(8,128)(2,1)S(1)}, bf16[1,1024,1024]{2,1,0:T(8,128)(2,1)}, u32[]{:S(2)}) copy-start(bf16[1,1024,1024]{2,1,0:T(8,128)(2,1)} %param.6) | copy-start | bytes 6291460
  9.3 2.0 %copy-start.1 = (bf16[1,2,128,1024]{3,2,1,0:T(8,128)(2,1)S(1)}, bf16[1,2,128,1024]{3,2,1,0:T(8,128)(2,1)}, u32[]{:S(2)}) copy-start(bf16[1,2,128,1024]{3,2,1,0:T(8,128)(2,1)} %param.7) | copy-start | bytes 1572868
  11.3 1.0 copy-start.3
  11.3 1.1 copy-start.4
  12.7 7.8 %collective-permute-start = (bf16[128,1024]{1,0:T(8,128)(2,1)S(1)}, bf16[128,1024]{1,0:T(8,128)(2,1)S(1)}, u32[]{:S(2)}, u32[]{:S(2)}) collective-permute-start(bf16[128,1024]{1,0:T(8,128)(2,1)S(1)} %fusion.87), channel_id=1, source_target_pairs={{128,0},{256,128},{384,256},{129,1},{257,129},{385,257},{130,2},{2... | collective-permute-start | bytes 786440 | tf_op jit(solution)/shard_map/ppermute | solution.py:10
  20.4 0.7 copy-start.5
  39.4 34.5 %all-to-all-start.1 = ((bf16[32,16,1024]{2,1,0:T(8,128)(2,1)}), bf16[32,16,1024]{2,1,0:T(8,128)(2,1)}, u32[]{:S(2)}, u32[]{:S(2)}) async-start(bf16[32,16,1024]{2,1,0:T(8,128)(2,1)} %bitcast.117), calls=%async_computation.1 | async-start | bytes 2097152 | tf_op jit(solution)/shard_map/all_to_all | solution.py:49
  75.3 9.6 %collective-permute-start.1 = (f32[16,1024]{1,0:T(8,128)S(1)}, f32[16,1024]{1,0:T(8,128)S(1)}, u32[]{:S(2)}, u32[]{:S(2)}) collective-permute-start(f32[16,1024]{1,0:T(8,128)S(1)} %convert_reduce_fusion), channel_id=1, source_target_pairs={{0,16},{16,0},{1,17},{17,1},{2,18},{18,2},{3,19},{19,3},{4,20},{20... | collective-permute-start | bytes 196616 | tf_op jit(solution)/shard_map/ppermute | solution.py:60
  84.8 9.4 %copy-start.2 = (bf16[2,128,1024]{2,1,0:T(8,128)(2,1)S(1)}, bf16[2,128,1024]{2,1,0:T(8,128)(2,1)}, u32[]{:S(2)}) copy-start(bf16[2,128,1024]{2,1,0:T(8,128)(2,1)} %param.9) | copy-start | bytes 1572868
  85.9 32.4 %all-to-all-start.2 = ((bf16[32,16,1024]{2,1,0:T(8,128)(2,1)}), bf16[32,16,1024]{2,1,0:T(8,128)(2,1)}, u32[]{:S(2)}, u32[]{:S(2)}) async-start(bf16[32,16,1024]{2,1,0:T(8,128)(2,1)} %broadcast_in_dim.12), calls=%async_computation.2 | async-start | bytes 2097152 | tf_op jit(solution)/shard_map/all_to_all | solution.py:49
  94.9 9.0 %collective-permute-start.2 = (bf16[128,1024]{1,0:T(8,128)(2,1)S(1)}, bf16[128,1024]{1,0:T(8,128)(2,1)S(1)}, u32[]{:S(2)}, u32[]{:S(2)}) collective-permute-start(bf16[128,1024]{1,0:T(8,128)(2,1)S(1)} %fusion.57), channel_id=1, source_target_pairs={{0,128},{128,256},{256,384},{1,129},{129,257},{257,385},{2,130},{1... | collective-permute-start | bytes 786440 | tf_op jit(solution)/shard_map/ppermute | solution.py:10

commit v2 on v0

v2 whole, which is shorter than its diff:
```python
import jax
import jax.numpy as jnp
from jax import lax
from jax.experimental import pallas as pl
from jax.experimental.pallas import tpu as pltpu
from jax.sharding import Mesh, PartitionSpec as P

DP = ("x", "y_hi", "z", "core")
REST = ("y_hi", "z")
F32, BF16 = jnp.float32, jnp.bfloat16
GELU_SCALE, GELU_CUBE = 0.7978845608028654, 0.044715


def normalize(rows):
    values = rows.astype(F32)
    centered = values - jnp.mean(values, axis=-1, keepdims=True)
    inverse = lax.rsqrt(jnp.mean(centered * centered, axis=-1, keepdims=True) + 1e-06)
    return centered * inverse, inverse


def gelu(value):
    bent = jnp.tanh(GELU_SCALE * (value + GELU_CUBE * value * value * value))
    return 0.5 * value * (1.0 + bent)


def gelu_slope(value):
    square = value * value
    bent = jnp.tanh(GELU_SCALE * value * (1.0 + GELU_CUBE * square))
    inner = GELU_SCALE * (1.0 + 3.0 * GELU_CUBE * square)
    return 0.5 * (1.0 + bent) + 0.5 * value * (1.0 - bent * bent) * inner


def matmul(left, right, dims):
    return lax.dot_general(left, right, ((dims[:1], dims[1:]), ((), ())), preferred_element_type=F32)


def input_gradient(pre_grad, matrix, upstream, normed, inverse):
    norm_grad = matmul(pre_grad, matrix, (1, 1))
    inner = norm_grad - jnp.mean(norm_grad, axis=-1, keepdims=True)
    inner = inner - normed * jnp.mean(norm_grad * normed, axis=-1, keepdims=True)
    return (upstream.astype(F32) + inverse * inner).astype(BF16)


def call(kernel, in_specs, out_specs, outs, flops, scratch=()):
    return pl.pallas_call(
        kernel,
        out_shape=[jax.ShapeDtypeStruct(shape, dtype) for shape, dtype in outs],
        grid_spec=pltpu.PrefetchScalarGridSpec(
            num_scalar_prefetch=0,
            grid=(1,),
            in_specs=in_specs,
            out_specs=out_specs,
            scratch_shapes=list(scratch),
        ),
        compiler_params=pltpu.CompilerParams(vmem_limit_bytes=16 << 20),
        cost_estimate=pl.CostEstimate(flops=flops, bytes_accessed=2 << 20, transcendentals=0),
    )


IN_PLACE = pl.BlockSpec(memory_space=pl.ANY)
TICKET = (8, 128)


def in_hbm(*arrays):
    return [pltpu.with_memory_space_constraint(array, pltpu.HBM) for array in arrays]


def whole(shape):
    return pl.BlockSpec(shape, lambda _: (0,) * len(shape))


def wholes(*shapes):
    return [whole(shape) for shape in shapes]


def of_step(step, rows):
    return pl.BlockSpec((1, *rows), lambda _: (step, 0, 0))


def halves(block):
    half = block.shape[1] // 2
    near, far = block[:, :half], block[:, half:]
    left = lax.axis_index("core") == 0
    return jnp.where(left, near, far), jnp.where(left, far, near)


def on_last_module():
    return lax.axis_index("module") == lax.axis_size("module") - 1


def first_backward(
    slots, replay, matrix, late, top, sent, rounded, pre_grad, rows0, rows1,
    slot_at, stored, weights, late_rows, top_rows, done,
):
    pairs = (
        (slots, slot_at),
        (replay.at[0], stored),
        (late.at[0], late_rows),
        (top.at[0], top_rows),
        (matrix.at[0], weights),
    )
    copies = [
        pltpu.make_async_copy(source, target, done.at[number])
        for number, (source, target) in enumerate(pairs)
    ]
    for copy in copies:
        copy.start()
    for copy in copies[:2]:
        copy.wait()
    rows0[...] = stored[slot_at[0, 0]]
    rows1[...] = stored[slot_at[0, 1]]
    normed, inverse = normalize(rows0[...])
    rounded[...] = normed.astype(BF16)
    for copy in copies[2:]:
        copy.wait()
    upstream = jnp.where(on_last_module(), top_rows[...], late_rows[...])
    preact = matmul(rounded[...], weights[...], (1, 0))
    pre_grad[...] = (upstream.astype(F32) * gelu_slope(preact)).astype(BF16)
    sent[...] = input_gradient(pre_grad[...], weights[...], upstream, normed, inverse)


def second_slope(rows1, rounded0, pre_first, matrix, after, slope, packed, kept):
    count, half = kept.shape
    normed, _ = normalize(rows1[...])
    rounded = normed.astype(BF16)
    packed[:count] = rounded0[...]
    packed[count : 2 * count] = rounded
    kept[...], away = halves(pre_first[...])
    packed[2 * count :, :half] = away[: count // 2]
    packed[2 * count :, half:] = away[count // 2 :]
    slope[...] = gelu_slope(matmul(rounded, matrix[0], (1, 0)))


def second_grads(slope, returning, top, delayed, pre_grad, kept, given):
    upstream = jnp.where(on_last_module(), top[0], returning[...])
    pre = (upstream.astype(F32) * slope[...]).astype(BF16)
    delayed[...] = upstream
    pre_grad[...] = pre
    kept[...], given[...] = halves(pre)


def weight_half(packed, kept0, kept1, pair, pair1, after, part):
    count, half = kept0.shape
    middle = count // 2
    total = matmul(packed[:count], kept0[...], (0, 0))
    total += matmul(packed[count : 2 * count], kept1[...], (0, 0))
    total += matmul(pair[:middle], pair[2 * count :, :half], (0, 0))
    total += matmul(pair[middle:count], pair[2 * count :, half:], (0, 0))
    total += matmul(pair[count : 2 * count], pair1[...], (0, 0))
    part[...] = total.astype(BF16)


def returned(rows1, pre_grad, matrix, delayed, after, result, ticket):
    normed, inverse = normalize(rows1[...])
    result[0] = input_gradient(pre_grad[...], matrix[0], delayed[...], normed, inverse)
    ticket[...] = jnp.zeros(TICKET, F32)


def fresh(rows, matrix):
    normed, _ = normalize(rows)
    preact = matmul(normed.astype(BF16), matrix, (1, 0))
    return (rows.astype(F32) + gelu(preact)).astype(BF16)


def fresh_first(stem, rows0, matrix, result):
    rows = jnp.where(lax.axis_index("module") == 0, stem[0], rows0[...])
    result[...] = fresh(rows, matrix[0])


def fresh_second(stem, arriving, matrix, after, result, ticket):
    rows = jnp.where(lax.axis_index("module") == 0, stem[0], arriving[...])
    result[0] = fresh(rows, matrix[0])
    ticket[...] = jnp.zeros(TICKET, F32)


def joined(own, other, ticket0, ticket1, result, done):
    half = own.shape[1]
    here = lax.axis_index("core")
    copies = [
        pltpu.make_async_copy(
            block, result.at[0, :, pl.ds(pl.multiple_of(core * half, half), half)], done.at[number]
        )
        for number, (block, core) in enumerate(((own, here), (other, 1 - here)))
    ]
    for copy in copies:
        copy.start()
    for copy in copies:
        copy.wait()


def shift(block, axis, distance):
    devices = range(lax.axis_size(axis))
    route = [(i - distance, i) for i in devices if i - distance in devices]
    return lax.ppermute(block, axis, route)


def swap(block, axis):
    return lax.ppermute(block, axis, [(0, 1), (1, 0)])


def exchange(block, axes):
    return lax.all_to_all(block, axes, 0, 0, tiled=True)


def per_device(weight, replay_buffer, slot_index, stem_input, top_grad, late_grad):
    steps, count, width = stem_input.shape
    half = width // 2
    rows, columns, packing = (count, width), (count, half), (2 * count + count // 2, width)
    matrix, one = (1, width, width), 2 * count * width * width

    sent, rounded0, pre_first, rows0, rows1 = call(
        first_backward,
        [IN_PLACE] * 5,
        wholes(*[rows] * 5),
        [(rows, BF16)] * 5,
        2 * one,
        scratch=[
            pltpu.SMEM(slot_index.shape, jnp.int32),
            pltpu.VMEM(replay_buffer.shape[1:], BF16),
            pltpu.VMEM((width, width), BF16),
            pltpu.VMEM(rows, BF16),
            pltpu.VMEM(rows, BF16),
            pltpu.SemaphoreType.DMA((5,)),
        ],
    )(*in_hbm(slot_index, replay_buffer, weight, late_grad, top_grad))
    returning = shift(sent, "module", -1)
    (first_out,) = call(
        fresh_first,
        [of_step(0, rows), *wholes(rows, matrix)],
        wholes(rows),
        [(rows, BF16)],
        one,
    )(stem_input, rows0, weight)
    arriving = shift(first_out, "module", 1)
    slope, packed, kept0 = call(
        second_slope,
        [*wholes(rows, rows, rows, matrix), IN_PLACE],
        wholes(rows, packing, columns),
        [(rows, F32), (packing, BF16), (columns, BF16)],
        one,
    )(rows1, rounded0, pre_first, weight, first_out)
    pair = swap(packed, "core")
    delayed, pre_second, kept1, given1 = call(
        second_grads,
        [*wholes(rows, rows), of_step(1, rows)],
        wholes(rows, rows, columns, columns),
        [(rows, BF16), (rows, BF16), (columns, BF16), (columns, BF16)],
        count * width,
    )(slope, returning, top_grad)
    (part,) = call(
        weight_half,
        [*wholes(packing, columns, columns, packing, columns), IN_PLACE],
        wholes((width, half)),
        [((width, half), BF16)],
        2 * one,
    )(packed, kept0, kept1, pair, swap(given1, "core"), arriving)

    outer, inner = lax.axis_size("x"), lax.axis_size(REST)
    block, piece = width // outer, width // outer // inner
    spread = exchange(part, "x").reshape(outer, block, half)
    spread = exchange(jnp.sum(spread.astype(F32), axis=0).astype(BF16), REST)
    spread = spread.reshape(inner, piece, half).astype(F32)
    grad_scale = float(steps * count * lax.axis_size(DP)) ** (-0.5)
    total = (jnp.sum(spread, axis=0) * grad_scale).astype(BF16)
    total = jnp.broadcast_to(total[None], (inner, piece, half)).reshape(block, half)
    total = exchange(total, REST)
    total = jnp.broadcast_to(total[None], (outer, block, half)).reshape(width, half)
    total = exchange(total, "x")
    other = swap(total, "core")

    sent_back, ticket0 = call(
        returned,
        [*wholes(rows, rows, matrix, rows), IN_PLACE],
        wholes((1, *rows), TICKET),
        [((1, *rows), BF16), (TICKET, F32)],
        one,
    )(rows1, pre_second, weight, delayed, total)
    handoff, ticket1 = call(
        fresh_second,
        [of_step(1, rows), *wholes(rows, matrix), IN_PLACE],
        wholes((1, *rows), TICKET),
        [((1, *rows), BF16), (TICKET, F32)],
        one,
    )(stem_input, arriving, weight, total)
    (weight_grad,) = call(
        joined,
        [IN_PLACE] * 4,
        [IN_PLACE],
        [(matrix, BF16)],
        count * width,
        scratch=[pltpu.SemaphoreType.DMA((2,))],
    )(total, other, ticket0, ticket1)
    return weight_grad, handoff, sent_back


def solution(mesh):
    modules, replicas = (mesh.shape[name] for name in ("module", "dp"))
    fine = Mesh(mesh.devices.reshape(modules, 4, 2, replicas // 16, 2), ("module", *DP))
    placed = (
        P("module", None, None),
        P("module", None, DP, None),
        P("module", None),
        P(None, DP, None),
        P(None, DP, None),
        P("module", DP, None),
    )
    return jax.shard_map(
        per_device,
        mesh=fine,
        in_specs=placed,
        out_specs=(P("module", None, None), P("module", DP, None), P("module", DP, None)),
        check_vma=False,
    )
```

time: 1620 us -> 115 us (0.07)
  waiting for transfers between devices: 1570 us -> 5.47 us
  blocking collectives: 0 us -> 71.8 us
  between operations: 18.1 us -> 0.82 us
    psum x1 -> x0, waiting for transfers between devices: 1560 us -> none  [per_device(): weight_grad = (lax.psum(summed, 'dp') * grad_scale).astype(jnp.bfloat16)]
    all_to_all x0 -> x4, blocking collectives: none -> 71.8 us  [exchange(): return lax.all_to_all(block, axes, 0, 0, tiled=True)]
    ppermute x2 -> x5, starting transfers between devices: 6.61 us -> 22.8 us  [the longest x3 17.5 us: swap(): return lax.ppermute(block, axis, [(0, 1), (1, 0)])]
  transfers between devices with their start and end apart: 3 -> 5, of which waited for: 3 -> 2; matrix products, arithmetic and copies ran while one was open for 0% -> 0% of each run, Pallas kernels for 0% -> 3%
where the time goes in v2:
time: 115 us
  blocking collectives  71.8 us (62%)
  starting transfers between devices  22.8 us (20%)
  Pallas kernels  11.3 us (10%)
  waiting for transfers between devices  5.47 us (5%)
  other arithmetic  2.2 us (2%)
    all_to_all x4, blocking collectives, exchange(): return lax.all_to_all(block, axes, 0, 0, tiled=True)  71.8 us
    ppermute x3, starting transfers between devices, swap(): return lax.ppermute(block, axis, [(0, 1), (1, 0)])  17.5 us
    ppermute x2, starting transfers between devices, shift(): return lax.ppermute(block, axis, route)  5.29 us
    ppermute x2, waiting for transfers between devices, shift(): return lax.ppermute(block, axis, route)  4.51 us
    pallas_call x1, Pallas kernels, per_device(): call(first_backward, [IN_PLACE] * 5, wholes(*[rows] * 5), [(rows, BF16)]...  3.65 us
  transfers between devices with their start and end apart: 5, of which 2 were waited for; matrix products, arithmetic and copies ran while one was open for 0% of the time, Pallas kernels for 3%

profile of v2, /device:TPU:1, one launch (start us, length us, event | category | flops | bytes accessed | tf_op | source)
XLA Modules:
  0.0 114.5 jit_solution(5899301206310626838)
XLA Ops:
  0.6 0.0 copy-start
  0.6 0.0 copy-start.1
  0.7 3.6 %shard_map.85 = (bf16[128,1024]{1,0:T(8,128)(2,1)S(1)}, bf16[128,1024]{1,0:T(8,128)(2,1)S(1)}, bf16[128,1024]{1,0:T(8,128)(2,1)S(1)}, bf16[128,1024]{1,0:T(8,128)(2,1)S(1)}, bf16[128,1024]{1,0:T(8,128)(2,1)S(1)}) custom-call(s32[1,2]{1,0:T(1,128)} %slots.1, bf16[1,2,128,1024]{3,2,1,0:T(8,128)(2,1)} %replay.1, bf16[1,1024,1024]{2,1,0:T(8,128)(2,1)} %matrix.9, ...), custom_call_target="tpu_custom_call" | custom-call | flops 536870912 | bytes 2097152 | tf_op jit(solution)/shard_map/pallas_call | solution.py:211
  4.3 0.0 copy-done
  4.3 0.0 copy-done.1
  4.3 0.7 shard_map.86.after
  5.0 0.0 copy-start.2
  5.0 0.9 shard_map.87
  5.9 8.8 %collective-permute-start.1 = (bf16[320,1024]{1,0:T(8,128)(2,1)S(1)}, bf16[320,1024]{1,0:T(8,128)(2,1)S(1)}, u32[]{:S(2)}, u32[]{:S(2)}) collective-permute-start(bf16[320,1024]{1,0:T(8,128)(2,1)S(1)} %get-tuple-element.23.packed), channel_id=1, source_target_pairs={{0,1},{1,0},{2,3},{3,2},{4,5},{5,4},{6,7},{7,6},{8,9},{9,8},{10,11... | collective-permute-start | bytes 1966088 | tf_op jit(solution)/shard_map/ppermute | solution.py:198
  14.7 1.3 %collective-permute-start = (bf16[128,1024]{1,0:T(8,128)(2,1)S(1)}, bf16[128,1024]{1,0:T(8,128)(2,1)S(1)}, u32[]{:S(2)}, u32[]{:S(2)}) collective-permute-start(bf16[128,1024]{1,0:T(8,128)(2,1)S(1)} %get-tuple-element.26), channel_id=1, source_target_pairs={{128,0},{256,128},{384,256},{129,1},{257,129},{385,257},{130,2},{2... | collective-permute-start | bytes 786440 | tf_op jit(solution)/shard_map/ppermute | solution.py:194
  16.0 4.0 %collective-permute-start.3 = (bf16[128,1024]{1,0:T(8,128)(2,1)S(1)}, bf16[128,1024]{1,0:T(8,128)(2,1)S(1)}, u32[]{:S(2)}, u32[]{:S(2)}) collective-permute-start(bf16[128,1024]{1,0:T(8,128)(2,1)S(1)} %shard_map.86.after), channel_id=1, source_target_pairs={{0,128},{128,256},{256,384},{1,129},{129,257},{257,385},{2,130},{1... | collective-permute-start | bytes 786440 | tf_op jit(solution)/shard_map/ppermute | solution.py:194
  20.0 4.5 %collective-permute-done.returning = bf16[128,1024]{1,0:T(8,128)(2,1)S(1)} collective-permute-done((bf16[128,1024]{1,0:T(8,128)(2,1)S(1)}, bf16[128,1024]{1,0:T(8,128)(2,1)S(1)}, u32[]{:S(2)}, u32[]{:S(2)}) %collective-permute-start) | collective-permute-done | bytes 262176 | tf_op jit(solution)/shard_map/ppermute | solution.py:194
  24.5 0.0 copy-done.2
  24.5 0.1 shard_map.88
  24.6 0.0 copy-start.3
  24.7 2.7 %collective-permute-start.2 = (bf16[128,512]{1,0:T(8,128)(2,1)S(1)}, bf16[128,512]{1,0:T(8,128)(2,1)S(1)}, u32[]{:S(2)}, u32[]{:S(2)}) collective-permute-start(bf16[128,512]{1,0:T(8,128)(2,1)S(1)} %get-tuple-element.28), channel_id=1, source_target_pairs={{0,1},{1,0},{2,3},{3,2},{4,5},{5,4},{6,7},{7,6},{8,9},{9,8},{10,11... | collective-permute-start | bytes 393224 | tf_op jit(solution)/shard_map/ppermute | solution.py:198
  27.4 0.0 collective-permute-done.3.after.arriving
  27.4 1.0 collective-permute-done.2.pair1
  28.3 0.0 collective-permute-done.1.pair
  28.3 1.5 %shard_map.89 = bf16[1024,512]{1,0:T(8,128)(2,1)S(1)} custom-call(bf16[320,1024]{1,0:T(8,128)(2,1)S(1)} %get-tuple-element.23.packed, bf16[128,512]{1,0:T(8,128)(2,1)S(1)} %get-tuple-element.24.kept0, bf16[128,512]{1,0:T(8,128)(2,1)S(1)} %get-tuple-element.27.kept1, bf16[320,1024]{1,0:T(8,128)(2,1)S(1)} %collective-permute-done.1.pair, ...), custom_call_target="tpu_custom_call" | custom-call | flops 536870912 | bytes 2097152 | tf_op jit(solution)/shard_map/pallas_call | solution.py:250
  29.9 18.0 %all_to_all.32 = bf16[4,256,512]{2,1,0:T(8,128)(2,1)} all-to-all(bf16[4,256,512]{2,1,0:T(8,128)(2,1)S(1)} %bitcast.8), channel_id=1, replica_groups=mesh['module'=4,'x'=4,'y_hi'=2,'z'=8,'core'=2] {'x'}, dimensions={0} | all-to-all | bytes 2097152 | tf_op jit(solution)/shard_map/all_to_all | solution.py:202
  47.9 2.2 %reduce_sum.21 = bf16[256,512]{1,0:T(8,128)(2,1)} reduce(bf16[4,256,512]{2,1,0:T(8,128)(2,1)} %all_to_all.32, bf16[]{:T(256)} %constant.1.clone.1), dimensions={0}, to_apply=%region_0.0 | reduce | flops 393216 | bytes 1310722 | tf_op jit(solution)/shard_map/reduce_sum | solution.py:261
  50.0 21.6 %all_to_all.33 = bf16[16,16,512]{2,1,0:T(8,128)(2,1)S(1)} all-to-all(bf16[16,16,512]{2,1,0:T(8,128)(2,1)} %bitcast.9), channel_id=1, replica_groups=mesh['module'=4,'x'=4,'y_hi'=2,'z'=8,'core'=2] {'y_hi','z'}, dimensions={0} | all-to-all | bytes 524288 | tf_op jit(solution)/shard_map/all_to_all | solution.py:202
  71.7 0.0 copy-start.4
  71.7 17.6 %all_to_all.34 = bf16[16,16,512]{2,1,0:T(8,128)(2,1)S(1)} all-to-all(bf16[16,16,512]{2,1,0:T(8,128)(2,1)S(1)} %broadcast_in_dim.6), channel_id=1, replica_groups=mesh['module'=4,'x'=4,'y_hi'=2,'z'=8,'core'=2] {'y_hi','z'}, dimensions={0} | all-to-all | bytes 524288 | tf_op jit(solution)/shard_map/all_to_all | solution.py:202
  89.4 0.1 broadcast_in_dim.16
  89.5 14.6 %all_to_all.35 = bf16[4,256,512]{2,1,0:T(8,128)(2,1)S(1)} all-to-all(bf16[4,256,512]{2,1,0:T(8,128)(2,1)S(1)} %broadcast_in_dim.16), channel_id=1, replica_groups=mesh['module'=4,'x'=4,'y_hi'=2,'z'=8,'core'=2] {'x'}, dimensions={0} | all-to-all | bytes 2097152 | tf_op jit(solution)/shard_map/all_to_all | solution.py:202
  104.0 6.0 %collective-permute-start.4 = (bf16[1024,512]{1,0:T(8,128)(2,1)S(1)}, bf16[1024,512]{1,0:T(8,128)(2,1)S(1)}, u32[]{:S(2)}, u32[]{:S(2)}) collective-permute-start(bf16[1024,512]{1,0:T(8,128)(2,1)S(1)} %bitcast.4), channel_id=1, source_target_pairs={{0,1},{1,0},{2,3},{3,2},{4,5},{5,4},{6,7},{7,6},{8,9},{9,8},{10,11... | collective-permute-start | bytes 3145736 | tf_op jit(solution)/shard_map/ppermute | solution.py:198
  110.1 1.7 %shard_map.90 = (bf16[1,128,1024]{2,1,0:T(8,128)(2,1)}, f32[8,128]{1,0:T(8,128)S(1)}) custom-call(bf16[128,1024]{1,0:T(8,128)(2,1)S(1)} %get-tuple-element.19.rows1, bf16[128,1024]{1,0:T(8,128)(2,1)S(1)} %copy-done.4, bf16[1,1024,1024]{2,1,0:T(8,128)(2,1)S(1)} %copy-done, bf16[128,1024]{1,0:T(8,128)(2,1)S(1)} %get-tuple-element.30.delayed, ...), custom_call_target="tpu_custom_call" | custom-call | flops 268435456 | bytes 2097152 | tf_op jit(solution)/shard_map/pallas_call | solution.py:271
  111.8 1.4 %shard_map.91 = (bf16[1,128,1024]{2,1,0:T(8,128)(2,1)}, f32[8,128]{1,0:T(8,128)S(1)}) custom-call(bf16[2,128,1024]{2,1,0:T(8,128)(2,1)S(1)} %copy-done.1, bf16[128,1024]{1,0:T(8,128)(2,1)S(1)} %collective-permute-done.3.after.arriving, bf16[1,1024,1024]{2,1,0:T(8,128)(2,1)S(1)} %copy-done, bf16[1024,512]{1,0:T(8,128)(2,1)S(1)} %bitcast.6), custom_call_target="tpu_custom_call" | custom-call | flops 268435456 | bytes 2097152 | tf_op jit(solution)/shard_map/pallas_call | solution.py:278
  113.2 0.0 collective-permute-done.4.other
  113.2 1.3 %shard_map.92 = bf16[1,1024,1024]{2,1,0:T(8,128)(2,1)} custom-call(bf16[1024,512]{1,0:T(8,128)(2,1)S(1)} %bitcast.7, bf16[1024,512]{1,0:T(8,128)(2,1)S(1)} %collective-permute-done.4.other, f32[8,128]{1,0:T(8,128)S(1)} %get-tuple-element.31.ticket0, f32[8,128]{1,0:T(8,128)S(1)} %get-tuple-element.32.ticket1), custom_call_target="tpu_custom_call" | custom-call | flops 131072 | bytes 2097152 | tf_op jit(solution)/shard_map/pallas_call | solution.py:285
  (5 shorter events, 0.1 us)
Async XLA Ops:
  0.6 3.7 %copy-start = (bf16[1,1024,1024]{2,1,0:T(8,128)(2,1)S(1)}, bf16[1,1024,1024]{2,1,0:T(8,128)(2,1)}, u32[]{:S(2)}) copy-start(bf16[1,1024,1024]{2,1,0:T(8,128)(2,1)} %matrix.9) | copy-start | bytes 6291460
  0.6 3.7 %copy-start.1 = (bf16[2,128,1024]{2,1,0:T(8,128)(2,1)S(1)}, bf16[2,128,1024]{2,1,0:T(8,128)(2,1)}, u32[]{:S(2)}) copy-start(bf16[2,128,1024]{2,1,0:T(8,128)(2,1)} %stem.3) | copy-start | bytes 1572868
  5.0 19.5 %copy-start.2 = (bf16[2,128,1024]{2,1,0:T(8,128)(2,1)S(1)}, bf16[2,128,1024]{2,1,0:T(8,128)(2,1)}, u32[]{:S(2)}) copy-start(bf16[2,128,1024]{2,1,0:T(8,128)(2,1)} %top.3) | copy-start | bytes 1572868
  5.9 22.4 %collective-permute-start.1 = (bf16[320,1024]{1,0:T(8,128)(2,1)S(1)}, bf16[320,1024]{1,0:T(8,128)(2,1)S(1)}, u32[]{:S(2)}, u32[]{:S(2)}) collective-permute-start(bf16[320,1024]{1,0:T(8,128)(2,1)S(1)} %get-tuple-element.23.packed), channel_id=1, source_target_pairs={{0,1},{1,0},{2,3},{3,2},{4,5},{5,4},{6,7},{7,6},{8,9},{9,8},{10,11... | collective-permute-start | bytes 1966088 | tf_op jit(solution)/shard_map/ppermute | solution.py:198
  14.7 9.8 %collective-permute-start = (bf16[128,1024]{1,0:T(8,128)(2,1)S(1)}, bf16[128,1024]{1,0:T(8,128)(2,1)S(1)}, u32[]{:S(2)}, u32[]{:S(2)}) collective-permute-start(bf16[128,1024]{1,0:T(8,128)(2,1)S(1)} %get-tuple-element.26), channel_id=1, source_target_pairs={{128,0},{256,128},{384,256},{129,1},{257,129},{385,257},{130,2},{2... | collective-permute-start | bytes 786440 | tf_op jit(solution)/shard_map/ppermute | solution.py:194
  16.0 11.4 %collective-permute-start.3 = (bf16[128,1024]{1,0:T(8,128)(2,1)S(1)}, bf16[128,1024]{1,0:T(8,128)(2,1)S(1)}, u32[]{:S(2)}, u32[]{:S(2)}) collective-permute-start(bf16[128,1024]{1,0:T(8,128)(2,1)S(1)} %shard_map.86.after), channel_id=1, source_target_pairs={{0,128},{128,256},{256,384},{1,129},{129,257},{257,385},{2,130},{1... | collective-permute-start | bytes 786440 | tf_op jit(solution)/shard_map/ppermute | solution.py:194
  24.6 5.2 %copy-start.3 = (bf16[128,1024]{1,0:T(8,128)(2,1)}, bf16[128,1024]{1,0:T(8,128)(2,1)S(1)}, u32[]{:S(2)}) copy-start(bf16[128,1024]{1,0:T(8,128)(2,1)S(1)} %get-tuple-element.29.pre_grad) | copy-start | bytes 786436
  24.7 3.7 %collective-permute-start.2 = (bf16[128,512]{1,0:T(8,128)(2,1)S(1)}, bf16[128,512]{1,0:T(8,128)(2,1)S(1)}, u32[]{:S(2)}, u32[]{:S(2)}) collective-permute-start(bf16[128,512]{1,0:T(8,128)(2,1)S(1)} %get-tuple-element.28), channel_id=1, source_target_pairs={{0,1},{1,0},{2,3},{3,2},{4,5},{5,4},{6,7},{7,6},{8,9},{9,8},{10,11... | collective-permute-start | bytes 393224 | tf_op jit(solution)/shard_map/ppermute | solution.py:198
  71.7 38.4 %copy-start.4 = (bf16[128,1024]{1,0:T(8,128)(2,1)S(1)}, bf16[128,1024]{1,0:T(8,128)(2,1)}, u32[]{:S(2)}) copy-start(bf16[128,1024]{1,0:T(8,128)(2,1)} %copy-done.3) | copy-start | bytes 786436
  104.0 9.2 %collective-permute-start.4 = (bf16[1024,512]{1,0:T(8,128)(2,1)S(1)}, bf16[1024,512]{1,0:T(8,128)(2,1)S(1)}, u32[]{:S(2)}, u32[]{:S(2)}) collective-permute-start(bf16[1024,512]{1,0:T(8,128)(2,1)S(1)} %bitcast.4), channel_id=1, source_target_pairs={{0,1},{1,0},{2,3},{3,2},{4,5},{5,4},{6,7},{7,6},{8,9},{9,8},{10,11... | collective-permute-start | bytes 3145736 | tf_op jit(solution)/shard_map/ppermute | solution.py:198

commit v3 on v2

--- a/solution.py
+++ b/solution.py
@@ -119,38 +119,35 @@
     sent[...] = input_gradient(pre_grad[...], weights[...], upstream, normed, inverse)
 
 
-def second_slope(rows1, rounded0, pre_first, matrix, after, slope, packed, kept):
-    count, half = kept.shape
+def second_slope(rows1, matrix, rounded1, slope):
     normed, _ = normalize(rows1[...])
-    rounded = normed.astype(BF16)
-    packed[:count] = rounded0[...]
-    packed[count : 2 * count] = rounded
-    kept[...], away = halves(pre_first[...])
-    packed[2 * count :, :half] = away[: count // 2]
-    packed[2 * count :, half:] = away[count // 2 :]
-    slope[...] = gelu_slope(matmul(rounded, matrix[0], (1, 0)))
-
-
-def second_grads(slope, returning, top, delayed, pre_grad, kept, given):
+    rounded1[...] = normed.astype(BF16)
+    slope[...] = gelu_slope(matmul(rounded1[...], matrix[0], (1, 0)))
+
+
+def second_grads(
+    rounded0, rounded1, pre_first, slope, returning, top, after, delayed, pre_grad, kept, packed
+):
+    count = rounded0.shape[0]
+    half = kept.shape[1]
     upstream = jnp.where(on_last_module(), top[0], returning[...])
     pre = (upstream.astype(F32) * slope[...]).astype(BF16)
     delayed[...] = upstream
     pre_grad[...] = pre
-    kept[...], given[...] = halves(pre)
-
-
-def weight_half(packed, kept0, kept1, pair, pair1, after, part):
-    count, half = kept0.shape
-    middle = count // 2
-    total = matmul(packed[:count], kept0[...], (0, 0))
-    total += matmul(packed[count : 2 * count], kept1[...], (0, 0))
-    total += matmul(pair[:middle], pair[2 * count :, :half], (0, 0))
-    total += matmul(pair[middle:count], pair[2 * count :, half:], (0, 0))
-    total += matmul(pair[count : 2 * count], pair1[...], (0, 0))
-    part[...] = total.astype(BF16)
-
-
-def returned(rows1, pre_grad, matrix, delayed, after, result, ticket):
+    packed[:count] = rounded0[...]
+    packed[count : 2 * count] = rounded1[...]
+    kept[:count], packed[2 * count :, :half] = halves(pre_first[...])
+    kept[count:], packed[2 * count :, half:] = halves(pre)
+
+
+def weight_half(packed, kept, pair, ticket, part):
+    count, half = kept.shape
+    given = jnp.concatenate([pair[count:, :half], pair[count:, half:]], axis=0)
+    total = matmul(packed[:count], kept[...], (0, 0))
+    part[...] = (total + matmul(pair[:count], given, (0, 0))).astype(BF16)
+
+
+def returned(rows1, pre_grad, matrix, delayed, result, ticket):
     normed, inverse = normalize(rows1[...])
     result[0] = input_gradient(pre_grad[...], matrix[0], delayed[...], normed, inverse)
     ticket[...] = jnp.zeros(TICKET, F32)
@@ -162,7 +159,7 @@
     return (rows.astype(F32) + gelu(preact)).astype(BF16)
 
 
-def fresh_first(stem, rows0, matrix, result):
+def fresh_first(stem, rows0, matrix, after, result):
     rows = jnp.where(lax.axis_index("module") == 0, stem[0], rows0[...])
     result[...] = fresh(rows, matrix[0])
 
@@ -173,7 +170,7 @@
     ticket[...] = jnp.zeros(TICKET, F32)
 
 
-def joined(own, other, ticket0, ticket1, result, done):
+def joined(own, other, ticket, result, done):
     half = own.shape[1]
     here = lax.axis_index("core")
     copies = [
@@ -205,7 +202,7 @@
 def per_device(weight, replay_buffer, slot_index, stem_input, top_grad, late_grad):
     steps, count, width = stem_input.shape
     half = width // 2
-    rows, columns, packing = (count, width), (count, half), (2 * count + count // 2, width)
+    rows, columns, packing = (count, width), (2 * count, half), (3 * count, width)
     matrix, one = (1, width, width), 2 * count * width * width
 
     sent, rounded0, pre_first, rows0, rows1 = call(
@@ -224,36 +221,43 @@
         ],
     )(*in_hbm(slot_index, replay_buffer, weight, late_grad, top_grad))
     returning = shift(sent, "module", -1)
+    rounded1, slope = call(
+        second_slope,
+        wholes(rows, matrix),
+        wholes(rows, rows),
+        [(rows, BF16), (rows, F32)],
+        one,
+    )(rows1, weight)
     (first_out,) = call(
         fresh_first,
-        [of_step(0, rows), *wholes(rows, matrix)],
+        [of_step(0, rows), *wholes(rows, matrix), IN_PLACE],
         wholes(rows),
         [(rows, BF16)],
         one,
-    )(stem_input, rows0, weight)
+    )(stem_input, rows0, weight, rounded1)
     arriving = shift(first_out, "module", 1)
-    slope, packed, kept0 = call(
-        second_slope,
-        [*wholes(rows, rows, rows, matrix), IN_PLACE],
-        wholes(rows, packing, columns),
-        [(rows, F32), (packing, BF16), (columns, BF16)],
+    delayed, pre_second, kept, packed = call(
+        second_grads,
+        [*wholes(*[rows] * 5), of_step(1, rows), IN_PLACE],
+        wholes(rows, rows, columns, packing),
+        [(rows, BF16), (rows, BF16), (columns, BF16), (packing, BF16)],
+        count * width,
+    )(rounded0, rounded1, pre_first, slope, returning, top_grad, arriving)
+    pair = swap(packed, "core")
+    sent_back, ticket = call(
+        returned,
+        wholes(rows, rows, matrix, rows),
+        wholes((1, *rows), TICKET),
+        [((1, *rows), BF16), (TICKET, F32)],
         one,
-    )(rows1, rounded0, pre_first, weight, first_out)
-    pair = swap(packed, "core")
-    delayed, pre_second, kept1, given1 = call(
-        second_grads,
-        [*wholes(rows, rows), of_step(1, rows)],
-        wholes(rows, rows, columns, columns),
-        [(rows, BF16), (rows, BF16), (columns, BF16), (columns, BF16)],
-        count * width,
-    )(slope, returning, top_grad)
+    )(rows1, pre_second, weight, delayed)
     (part,) = call(
         weight_half,
-        [*wholes(packing, columns, columns, packing, columns), IN_PLACE],
+        [*wholes(packing, columns, packing), IN_PLACE],
         wholes((width, half)),
         [((width, half), BF16)],
         2 * one,
-    )(packed, kept0, kept1, pair, swap(given1, "core"), arriving)
+    )(packed, kept, pair, ticket)
 
     outer, inner = lax.axis_size("x"), lax.axis_size(REST)
     block, piece = width // outer, width // outer // inner
@@ -268,28 +272,21 @@
     total = exchange(total, "x")
     other = swap(total, "core")
 
-    sent_back, ticket0 = call(
-        returned,
-        [*wholes(rows, rows, matrix, rows), IN_PLACE],
-        wholes((1, *rows), TICKET),
-        [((1, *rows), BF16), (TICKET, F32)],
-        one,
-    )(rows1, pre_second, weight, delayed, total)
-    handoff, ticket1 = call(
+    handoff, ticket = call(
         fresh_second,
         [of_step(1, rows), *wholes(rows, matrix), IN_PLACE],
         wholes((1, *rows), TICKET),
         [((1, *rows), BF16), (TICKET, F32)],
         one,
-    )(stem_input, arriving, weight, total)
+    )(stem_input, arriving, *in_hbm(weight), total)
     (weight_grad,) = call(
         joined,
-        [IN_PLACE] * 4,
+        [IN_PLACE] * 3,
         [IN_PLACE],
         [(matrix, BF16)],
         count * width,
         scratch=[pltpu.SemaphoreType.DMA((2,))],
-    )(total, other, ticket0, ticket1)
+    )(total, other, ticket)
     return weight_grad, handoff, sent_back
 
 

time: 115 us -> 113 us (0.983); the launches traced: 115 us -> 111 us
  blocking collectives: 71.8 us -> 74.3 us
  starting transfers between devices: 22.8 us -> 20.3 us
  waiting for transfers between devices: 5.47 us -> 3.46 us
  other arithmetic: 2.2 us -> 0.29 us
    ppermute x3 -> x2, starting transfers between devices: 17.5 us -> 14.4 us  [swap(): return lax.ppermute(block, axis, [(0, 1), (1, 0)])]
    all_to_all x4, blocking collectives: 71.8 us -> 74.3 us  [exchange(): return lax.all_to_all(block, axes, 0, 0, tiled=True)]
    reduce_sum x1, other arithmetic: 2.15 us -> 0.24 us  [per_device(): spread = exchange(jnp.sum(spread.astype(F32), axis=0).astype(BF16), REST)]
    pallas_call x1, Pallas kernels: 1.4 us -> 2.98 us  [per_device(): call(fresh_second, [of_step(1, rows), *wholes(rows, matrix), IN_PLACE], w...]
    ppermute x2, waiting for transfers between devices: 4.51 us -> 3.28 us  [shift(): return lax.ppermute(block, axis, route)]
  transfers between devices with their start and end apart: 5 -> 4, of which waited for: 2 -> 3; matrix products, arithmetic and copies ran while one was open for 0% -> 0% of each run, Pallas kernels for 3% -> 6%
where the time goes in v3:
time: 113 us; the launch traced here: 111 us
  blocking collectives  74.3 us (66%)
  starting transfers between devices  20.3 us (18%)
  Pallas kernels  12.1 us (11%)
  waiting for transfers between devices  3.46 us (3%)
    all_to_all x4, blocking collectives, exchange(): return lax.all_to_all(block, axes, 0, 0, tiled=True)  74.3 us
    ppermute x2, starting transfers between devices, swap(): return lax.ppermute(block, axis, [(0, 1), (1, 0)])  14.4 us
    ppermute x2, starting transfers between devices, shift(): return lax.ppermute(block, axis, route)  5.98 us
    pallas_call x1, Pallas kernels, per_device(): call(first_backward, [IN_PLACE] * 5, wholes(*[rows] * 5), [(rows, BF16)]...  3.64 us
    ppermute x2, waiting for transfers between devices, shift(): return lax.ppermute(block, axis, route)  3.28 us
    pallas_call x1, Pallas kernels, per_device(): call(fresh_second, [of_step(1, rows), *wholes(rows, matrix), IN_PLACE], w...  2.98 us
  transfers between devices with their start and end apart: 4, of which 3 were waited for; matrix products, arithmetic and copies ran while one was open for 0% of the time, Pallas kernels for 6%

profile of v3, /device:TPU:1, one launch (start us, length us, event | category | flops | bytes accessed | tf_op | source)
XLA Modules:
  0.0 111.4 jit_solution(5276745853194272558)
XLA Ops:
  0.6 0.0 copy-start
  0.6 0.0 copy-start.1
  0.7 3.6 %shard_map.85 = (bf16[128,1024]{1,0:T(8,128)(2,1)S(1)}, bf16[128,1024]{1,0:T(8,128)(2,1)S(1)}, bf16[128,1024]{1,0:T(8,128)(2,1)S(1)}, bf16[128,1024]{1,0:T(8,128)(2,1)S(1)}, bf16[128,1024]{1,0:T(8,128)(2,1)S(1)}) custom-call(s32[1,2]{1,0:T(1,128)} %slots.1, bf16[1,2,128,1024]{3,2,1,0:T(8,128)(2,1)} %replay.1, bf16[1,1024,1024]{2,1,0:T(8,128)(2,1)} %matrix.9, ...), custom_call_target="tpu_custom_call" | custom-call | flops 536870912 | bytes 2097152 | tf_op jit(solution)/shard_map/pallas_call | solution.py:208
  4.3 1.3 %collective-permute-start = (bf16[128,1024]{1,0:T(8,128)(2,1)S(1)}, bf16[128,1024]{1,0:T(8,128)(2,1)S(1)}, u32[]{:S(2)}, u32[]{:S(2)}) collective-permute-start(bf16[128,1024]{1,0:T(8,128)(2,1)S(1)} %get-tuple-element.23), channel_id=1, source_target_pairs={{128,0},{256,128},{384,256},{129,1},{257,129},{385,257},{130,2},{2... | collective-permute-start | bytes 786440 | tf_op jit(solution)/shard_map/ppermute | solution.py:191
  5.6 0.0 copy-done
  5.6 0.8 shard_map.86
  6.4 0.0 copy-start.2
  6.5 0.0 copy-done.1
  6.5 0.7 shard_map.87
  7.2 4.7 %collective-permute-start.1 = (bf16[128,1024]{1,0:T(8,128)(2,1)S(1)}, bf16[128,1024]{1,0:T(8,128)(2,1)S(1)}, u32[]{:S(2)}, u32[]{:S(2)}) collective-permute-start(bf16[128,1024]{1,0:T(8,128)(2,1)S(1)} %shard_map.87), channel_id=1, source_target_pairs={{0,128},{128,256},{256,384},{1,129},{129,257},{257,385},{2,130},{1... | collective-permute-start | bytes 786440 | tf_op jit(solution)/shard_map/ppermute | solution.py:191
  11.9 0.2 collective-permute-done.returning
  12.1 3.1 %collective-permute-done.1.after.arriving = bf16[128,1024]{1,0:T(8,128)(2,1)S(1)} collective-permute-done((bf16[128,1024]{1,0:T(8,128)(2,1)S(1)}, bf16[128,1024]{1,0:T(8,128)(2,1)S(1)}, u32[]{:S(2)}, u32[]{:S(2)}) %collective-permute-start.1) | collective-permute-done | bytes 262176 | tf_op jit(solution)/shard_map/ppermute | solution.py:191
  15.1 0.0 copy-done.2
  15.2 0.1 shard_map.88
  15.3 9.2 %collective-permute-start.2 = (bf16[384,1024]{1,0:T(8,128)(2,1)S(1)}, bf16[384,1024]{1,0:T(8,128)(2,1)S(1)}, u32[]{:S(2)}, u32[]{:S(2)}) collective-permute-start(bf16[384,1024]{1,0:T(8,128)(2,1)S(1)} %get-tuple-element.25.packed), channel_id=1, source_target_pairs={{0,1},{1,0},{2,3},{3,2},{4,5},{5,4},{6,7},{7,6},{8,9},{9,8},{10,11... | collective-permute-start | bytes 2359304 | tf_op jit(solution)/shard_map/ppermute | solution.py:195
  24.6 1.7 %shard_map.89 = (bf16[1,128,1024]{2,1,0:T(8,128)(2,1)}, f32[8,128]{1,0:T(8,128)S(1)}) custom-call(bf16[128,1024]{1,0:T(8,128)(2,1)S(1)} %get-tuple-element.19.rows1, bf16[128,1024]{1,0:T(8,128)(2,1)S(1)} %get-tuple-element.27.pre_grad, bf16[1,1024,1024]{2,1,0:T(8,128)(2,1)S(1)} %copy-done, bf16[128,1024]{1,0:T(8,128)(2,1)S(1)} %get-tuple-element.28.delayed), custom_call_target="tpu_custom_call" | custom-call | flops 268435456 | bytes 2097152 | tf_op jit(solution)/shard_map/pallas_call | solution.py:247
  26.3 0.2 collective-permute-done.2.pair
  26.4 0.7 shard_map.90
  27.2 17.3 %all_to_all.32 = bf16[4,256,512]{2,1,0:T(8,128)(2,1)S(1)} all-to-all(bf16[4,256,512]{2,1,0:T(8,128)(2,1)S(1)} %bitcast.7), channel_id=1, replica_groups=mesh['module'=4,'x'=4,'y_hi'=2,'z'=8,'core'=2] {'x'}, dimensions={0} | all-to-all | bytes 2097152 | tf_op jit(solution)/shard_map/all_to_all | solution.py:199
  44.5 0.2 reduce_sum.21
  44.7 23.5 %all_to_all.33 = bf16[16,16,512]{2,1,0:T(8,128)(2,1)S(1)} all-to-all(bf16[16,16,512]{2,1,0:T(8,128)(2,1)S(1)} %bitcast.8), channel_id=1, replica_groups=mesh['module'=4,'x'=4,'y_hi'=2,'z'=8,'core'=2] {'y_hi','z'}, dimensions={0} | all-to-all | bytes 524288 | tf_op jit(solution)/shard_map/all_to_all | solution.py:199
  68.3 18.3 %all_to_all.34 = bf16[16,16,512]{2,1,0:T(8,128)(2,1)S(1)} all-to-all(bf16[16,16,512]{2,1,0:T(8,128)(2,1)S(1)} %broadcast_in_dim.6), channel_id=1, replica_groups=mesh['module'=4,'x'=4,'y_hi'=2,'z'=8,'core'=2] {'y_hi','z'}, dimensions={0} | all-to-all | bytes 524288 | tf_op jit(solution)/shard_map/all_to_all | solution.py:199
  86.6 0.1 broadcast_in_dim.16
  86.7 15.3 %all_to_all.35 = bf16[4,256,512]{2,1,0:T(8,128)(2,1)S(1)} all-to-all(bf16[4,256,512]{2,1,0:T(8,128)(2,1)S(1)} %broadcast_in_dim.16), channel_id=1, replica_groups=mesh['module'=4,'x'=4,'y_hi'=2,'z'=8,'core'=2] {'x'}, dimensions={0} | all-to-all | bytes 2097152 | tf_op jit(solution)/shard_map/all_to_all | solution.py:199
  101.9 5.1 %collective-permute-start.3 = (bf16[1024,512]{1,0:T(8,128)(2,1)S(1)}, bf16[1024,512]{1,0:T(8,128)(2,1)S(1)}, u32[]{:S(2)}, u32[]{:S(2)}) collective-permute-start(bf16[1024,512]{1,0:T(8,128)(2,1)S(1)} %bitcast.4), channel_id=1, source_target_pairs={{0,1},{1,0},{2,3},{3,2},{4,5},{5,4},{6,7},{7,6},{8,9},{9,8},{10,11... | collective-permute-start | bytes 3145736 | tf_op jit(solution)/shard_map/ppermute | solution.py:195
  107.1 3.0 %shard_map.91 = (bf16[1,128,1024]{2,1,0:T(8,128)(2,1)}, f32[8,128]{1,0:T(8,128)S(1)}) custom-call(bf16[2,128,1024]{2,1,0:T(8,128)(2,1)S(1)} %copy-done.1, bf16[128,1024]{1,0:T(8,128)(2,1)S(1)} %collective-permute-done.1.after.arriving, bf16[1,1024,1024]{2,1,0:T(8,128)(2,1)} %matrix.9, bf16[1024,512]{1,0:T(8,128)(2,1)S(1)} %bitcast.5), custom_call_target="tpu_custom_call" | custom-call | flops 268435456 | bytes 2097152 | tf_op jit(solution)/shard_map/pallas_call | solution.py:275
  110.0 0.0 collective-permute-done.3.other
  110.0 1.3 %shard_map.92 = bf16[1,1024,1024]{2,1,0:T(8,128)(2,1)} custom-call(bf16[1024,512]{1,0:T(8,128)(2,1)S(1)} %bitcast.6, bf16[1024,512]{1,0:T(8,128)(2,1)S(1)} %collective-permute-done.3.other, f32[8,128]{1,0:T(8,128)S(1)} %get-tuple-element.30.ticket), custom_call_target="tpu_custom_call" | custom-call | flops 131072 | bytes 2097152 | tf_op jit(solution)/shard_map/pallas_call | solution.py:282
  (3 shorter events, 0.1 us)
Async XLA Ops:
  0.6 5.0 %copy-start = (bf16[1,1024,1024]{2,1,0:T(8,128)(2,1)S(1)}, bf16[1,1024,1024]{2,1,0:T(8,128)(2,1)}, u32[]{:S(2)}) copy-start(bf16[1,1024,1024]{2,1,0:T(8,128)(2,1)} %matrix.9) | copy-start | bytes 6291460
  0.6 5.8 %copy-start.1 = (bf16[2,128,1024]{2,1,0:T(8,128)(2,1)S(1)}, bf16[2,128,1024]{2,1,0:T(8,128)(2,1)}, u32[]{:S(2)}) copy-start(bf16[2,128,1024]{2,1,0:T(8,128)(2,1)} %stem.3) | copy-start | bytes 1572868
  4.3 7.8 %collective-permute-start = (bf16[128,1024]{1,0:T(8,128)(2,1)S(1)}, bf16[128,1024]{1,0:T(8,128)(2,1)S(1)}, u32[]{:S(2)}, u32[]{:S(2)}) collective-permute-start(bf16[128,1024]{1,0:T(8,128)(2,1)S(1)} %get-tuple-element.23), channel_id=1, source_target_pairs={{128,0},{256,128},{384,256},{129,1},{257,129},{385,257},{130,2},{2... | collective-permute-start | bytes 786440 | tf_op jit(solution)/shard_map/ppermute | solution.py:191
  6.4 8.7 %copy-start.2 = (bf16[2,128,1024]{2,1,0:T(8,128)(2,1)S(1)}, bf16[2,128,1024]{2,1,0:T(8,128)(2,1)}, u32[]{:S(2)}) copy-start(bf16[2,128,1024]{2,1,0:T(8,128)(2,1)} %top.3) | copy-start | bytes 1572868
  7.2 8.0 %collective-permute-start.1 = (bf16[128,1024]{1,0:T(8,128)(2,1)S(1)}, bf16[128,1024]{1,0:T(8,128)(2,1)S(1)}, u32[]{:S(2)}, u32[]{:S(2)}) collective-permute-start(bf16[128,1024]{1,0:T(8,128)(2,1)S(1)} %shard_map.87), channel_id=1, source_target_pairs={{0,128},{128,256},{256,384},{1,129},{129,257},{257,385},{2,130},{1... | collective-permute-start | bytes 786440 | tf_op jit(solution)/shard_map/ppermute | solution.py:191
  15.3 11.1 %collective-permute-start.2 = (bf16[384,1024]{1,0:T(8,128)(2,1)S(1)}, bf16[384,1024]{1,0:T(8,128)(2,1)S(1)}, u32[]{:S(2)}, u32[]{:S(2)}) collective-permute-start(bf16[384,1024]{1,0:T(8,128)(2,1)S(1)} %get-tuple-element.25.packed), channel_id=1, source_target_pairs={{0,1},{1,0},{2,3},{3,2},{4,5},{5,4},{6,7},{7,6},{8,9},{9,8},{10,11... | collective-permute-start | bytes 2359304 | tf_op jit(solution)/shard_map/ppermute | solution.py:195
  101.9 8.1 %collective-permute-start.3 = (bf16[1024,512]{1,0:T(8,128)(2,1)S(1)}, bf16[1024,512]{1,0:T(8,128)(2,1)S(1)}, u32[]{:S(2)}, u32[]{:S(2)}) collective-permute-start(bf16[1024,512]{1,0:T(8,128)(2,1)S(1)} %bitcast.4), channel_id=1, source_target_pairs={{0,1},{1,0},{2,3},{3,2},{4,5},{5,4},{6,7},{7,6},{8,9},{9,8},{10,11... | collective-permute-start | bytes 3145736 | tf_op jit(solution)/shard_map/ppermute | solution.py:195

commit v4 on v3

--- a/solution.py
+++ b/solution.py
@@ -53,7 +53,7 @@
             scratch_shapes=list(scratch),
         ),
         compiler_params=pltpu.CompilerParams(vmem_limit_bytes=16 << 20),
-        cost_estimate=pl.CostEstimate(flops=flops, bytes_accessed=2 << 20, transcendentals=0),
+        cost_estimate=pl.CostEstimate(flops=flops, bytes_accessed=flops // 64, transcendentals=0),
     )
 
 
@@ -126,7 +126,7 @@
 
 
 def second_grads(
-    rounded0, rounded1, pre_first, slope, returning, top, after, delayed, pre_grad, kept, packed
+    rounded0, rounded1, pre_first, slope, returning, top, delayed, pre_grad, kept, packed
 ):
     count = rounded0.shape[0]
     half = kept.shape[1]
@@ -145,6 +145,10 @@
     given = jnp.concatenate([pair[count:, :half], pair[count:, half:]], axis=0)
     total = matmul(packed[:count], kept[...], (0, 0))
     part[...] = (total + matmul(pair[:count], given, (0, 0))).astype(BF16)
+
+
+def marker(ticket, after, result):
+    result[...] = ticket[...]
 
 
 def returned(rows1, pre_grad, matrix, delayed, result, ticket):
@@ -238,19 +242,22 @@
     arriving = shift(first_out, "module", 1)
     delayed, pre_second, kept, packed = call(
         second_grads,
-        [*wholes(*[rows] * 5), of_step(1, rows), IN_PLACE],
+        [*wholes(*[rows] * 5), of_step(1, rows)],
         wholes(rows, rows, columns, packing),
         [(rows, BF16), (rows, BF16), (columns, BF16), (packing, BF16)],
         count * width,
-    )(rounded0, rounded1, pre_first, slope, returning, top_grad, arriving)
+    )(rounded0, rounded1, pre_first, slope, returning, top_grad)
     pair = swap(packed, "core")
     sent_back, ticket = call(
         returned,
         wholes(rows, rows, matrix, rows),
         wholes((1, *rows), TICKET),
         [((1, *rows), BF16), (TICKET, F32)],
-        one,
+        count,
     )(rows1, pre_second, weight, delayed)
+    (ticket,) = call(
+        marker, [whole(TICKET), IN_PLACE], wholes(TICKET), [(TICKET, F32)], 100000000000
+    )(ticket, arriving)
     (part,) = call(
         weight_half,
         [*wholes(packing, columns, packing), IN_PLACE],

time: 113 us -> 108 us (0.956); the launches traced: 111 us -> 108 us
  waiting for transfers between devices: 3.46 us -> 0.4 us
  blocking collectives: 74.3 us -> 72.3 us
  starting transfers between devices: 20.3 us -> 21.8 us
    ppermute x2, waiting for transfers between devices: 3.28 us -> 0.23 us  [shift(): return lax.ppermute(block, axis, route)]
    all_to_all x4, blocking collectives: 74.3 us -> 72.3 us  [exchange(): return lax.all_to_all(block, axes, 0, 0, tiled=True)]
    ppermute x2, starting transfers between devices: 14.4 us -> 15.8 us  [swap(): return lax.ppermute(block, axis, [(0, 1), (1, 0)])]
  transfers between devices with their start and end apart: 4 -> 4, of which waited for: 3 -> 2; matrix products, arithmetic and copies ran while one was open for 0% -> 0% of each run, Pallas kernels for 6% -> 6%
where the time goes in v4:
time: 108 us
  blocking collectives  72.3 us (67%)
  starting transfers between devices  21.8 us (20%)
  Pallas kernels  12.1 us (11%)
    all_to_all x4, blocking collectives, exchange(): return lax.all_to_all(block, axes, 0, 0, tiled=True)  72.3 us
    ppermute x2, starting transfers between devices, swap(): return lax.ppermute(block, axis, [(0, 1), (1, 0)])  15.8 us
    ppermute x2, starting transfers between devices, shift(): return lax.ppermute(block, axis, route)  5.98 us
    pallas_call x1, Pallas kernels, per_device(): call(first_backward, [IN_PLACE] * 5, wholes(*[rows] * 5), [(rows, BF16)]...  3.64 us
    pallas_call x1, Pallas kernels, per_device(): call(fresh_second, [of_step(1, rows), *wholes(rows, matrix), IN_PLACE], w...  2.98 us
  transfers between devices with their start and end apart: 4, of which 2 were waited for; matrix products, arithmetic and copies ran while one was open for 0% of the time, Pallas kernels for 6%

profile of v4, /device:TPU:1, one launch (start us, length us, event | category | flops | bytes accessed | tf_op | source)
XLA Modules:
  0.0 107.8 jit_solution(10854080980632163853)
XLA Ops:
  0.6 0.0 copy-start
  0.6 0.0 copy-start.1
  0.7 3.6 %shard_map.85 = (bf16[128,1024]{1,0:T(8,128)(2,1)S(1)}, bf16[128,1024]{1,0:T(8,128)(2,1)S(1)}, bf16[128,1024]{1,0:T(8,128)(2,1)S(1)}, bf16[128,1024]{1,0:T(8,128)(2,1)S(1)}, bf16[128,1024]{1,0:T(8,128)(2,1)S(1)}) custom-call(s32[1,2]{1,0:T(1,128)} %slots.1, bf16[1,2,128,1024]{3,2,1,0:T(8,128)(2,1)} %replay.1, bf16[1,1024,1024]{2,1,0:T(8,128)(2,1)} %matrix.9, ...), custom_call_target="tpu_custom_call" | custom-call | flops 536870912 | bytes 8388608 | tf_op jit(solution)/shard_map/pallas_call | solution.py:212
  4.3 1.3 %collective-permute-start = (bf16[128,1024]{1,0:T(8,128)(2,1)S(1)}, bf16[128,1024]{1,0:T(8,128)(2,1)S(1)}, u32[]{:S(2)}, u32[]{:S(2)}) collective-permute-start(bf16[128,1024]{1,0:T(8,128)(2,1)S(1)} %get-tuple-element.23), channel_id=1, source_target_pairs={{128,0},{256,128},{384,256},{129,1},{257,129},{385,257},{130,2},{2... | collective-permute-start | bytes 786440 | tf_op jit(solution)/shard_map/ppermute | solution.py:195
  5.6 0.0 copy-done
  5.6 0.8 shard_map.86
  6.4 0.0 copy-start.2
  6.5 0.0 copy-done.1
  6.5 0.7 shard_map.89
  7.2 4.7 %collective-permute-start.2 = (bf16[128,1024]{1,0:T(8,128)(2,1)S(1)}, bf16[128,1024]{1,0:T(8,128)(2,1)S(1)}, u32[]{:S(2)}, u32[]{:S(2)}) collective-permute-start(bf16[128,1024]{1,0:T(8,128)(2,1)S(1)} %shard_map.89), channel_id=1, source_target_pairs={{0,128},{128,256},{256,384},{1,129},{129,257},{257,385},{2,130},{1... | collective-permute-start | bytes 786440 | tf_op jit(solution)/shard_map/ppermute | solution.py:195
  11.9 0.2 collective-permute-done.returning
  12.1 0.0 copy-done.2
  12.1 0.1 shard_map.87
  12.3 9.3 %collective-permute-start.1 = (bf16[384,1024]{1,0:T(8,128)(2,1)S(1)}, bf16[384,1024]{1,0:T(8,128)(2,1)S(1)}, u32[]{:S(2)}, u32[]{:S(2)}) collective-permute-start(bf16[384,1024]{1,0:T(8,128)(2,1)S(1)} %get-tuple-element.24.packed), channel_id=1, source_target_pairs={{0,1},{1,0},{2,3},{3,2},{4,5},{5,4},{6,7},{7,6},{8,9},{9,8},{10,11... | collective-permute-start | bytes 2359304 | tf_op jit(solution)/shard_map/ppermute | solution.py:199
  21.5 1.7 %shard_map.88 = (bf16[1,128,1024]{2,1,0:T(8,128)(2,1)}, f32[8,128]{1,0:T(8,128)S(1)}) custom-call(bf16[128,1024]{1,0:T(8,128)(2,1)S(1)} %get-tuple-element.19.rows1, bf16[128,1024]{1,0:T(8,128)(2,1)S(1)} %get-tuple-element.26.pre_grad, bf16[1,1024,1024]{2,1,0:T(8,128)(2,1)S(1)} %copy-done, bf16[128,1024]{1,0:T(8,128)(2,1)S(1)} %get-tuple-element.27.delayed), custom_call_target="tpu_custom_call" | custom-call | flops 128 | bytes 2 | tf_op jit(solution)/shard_map/pallas_call | solution.py:251
  23.2 0.0 collective-permute-done.2.after.arriving
  23.3 0.2 collective-permute-done.1.pair
  23.4 0.7 shard_map.91
  24.2 17.3 %all_to_all.32 = bf16[4,256,512]{2,1,0:T(8,128)(2,1)S(1)} all-to-all(bf16[4,256,512]{2,1,0:T(8,128)(2,1)S(1)} %bitcast.7), channel_id=1, replica_groups=mesh['module'=4,'x'=4,'y_hi'=2,'z'=8,'core'=2] {'x'}, dimensions={0} | all-to-all | bytes 2097152 | tf_op jit(solution)/shard_map/all_to_all | solution.py:203
  41.4 0.2 reduce_sum.21
  41.7 23.7 %all_to_all.33 = bf16[16,16,512]{2,1,0:T(8,128)(2,1)S(1)} all-to-all(bf16[16,16,512]{2,1,0:T(8,128)(2,1)S(1)} %bitcast.8), channel_id=1, replica_groups=mesh['module'=4,'x'=4,'y_hi'=2,'z'=8,'core'=2] {'y_hi','z'}, dimensions={0} | all-to-all | bytes 524288 | tf_op jit(solution)/shard_map/all_to_all | solution.py:203
  65.5 17.5 %all_to_all.34 = bf16[16,16,512]{2,1,0:T(8,128)(2,1)S(1)} all-to-all(bf16[16,16,512]{2,1,0:T(8,128)(2,1)S(1)} %broadcast_in_dim.6), channel_id=1, replica_groups=mesh['module'=4,'x'=4,'y_hi'=2,'z'=8,'core'=2] {'y_hi','z'}, dimensions={0} | all-to-all | bytes 524288 | tf_op jit(solution)/shard_map/all_to_all | solution.py:203
  83.0 0.1 broadcast_in_dim.16
  83.1 13.8 %all_to_all.35 = bf16[4,256,512]{2,1,0:T(8,128)(2,1)S(1)} all-to-all(bf16[4,256,512]{2,1,0:T(8,128)(2,1)S(1)} %broadcast_in_dim.16), channel_id=1, replica_groups=mesh['module'=4,'x'=4,'y_hi'=2,'z'=8,'core'=2] {'x'}, dimensions={0} | all-to-all | bytes 2097152 | tf_op jit(solution)/shard_map/all_to_all | solution.py:203
  96.9 6.5 %collective-permute-start.3 = (bf16[1024,512]{1,0:T(8,128)(2,1)S(1)}, bf16[1024,512]{1,0:T(8,128)(2,1)S(1)}, u32[]{:S(2)}, u32[]{:S(2)}) collective-permute-start(bf16[1024,512]{1,0:T(8,128)(2,1)S(1)} %bitcast.4), channel_id=1, source_target_pairs={{0,1},{1,0},{2,3},{3,2},{4,5},{5,4},{6,7},{7,6},{8,9},{9,8},{10,11... | collective-permute-start | bytes 3145736 | tf_op jit(solution)/shard_map/ppermute | solution.py:199
  103.4 3.0 %shard_map.92 = (bf16[1,128,1024]{2,1,0:T(8,128)(2,1)}, f32[8,128]{1,0:T(8,128)S(1)}) custom-call(bf16[2,128,1024]{2,1,0:T(8,128)(2,1)S(1)} %copy-done.1, bf16[128,1024]{1,0:T(8,128)(2,1)S(1)} %collective-permute-done.2.after.arriving, bf16[1,1024,1024]{2,1,0:T(8,128)(2,1)} %matrix.9, bf16[1024,512]{1,0:T(8,128)(2,1)S(1)} %bitcast.5), custom_call_target="tpu_custom_call" | custom-call | flops 268435456 | bytes 4194304 | tf_op jit(solution)/shard_map/pallas_call | solution.py:282
  106.4 0.0 collective-permute-done.3.other
  106.4 1.3 %shard_map.93 = bf16[1,1024,1024]{2,1,0:T(8,128)(2,1)} custom-call(bf16[1024,512]{1,0:T(8,128)(2,1)S(1)} %bitcast.6, bf16[1024,512]{1,0:T(8,128)(2,1)S(1)} %collective-permute-done.3.other, f32[8,128]{1,0:T(8,128)S(1)} %get-tuple-element.30.ticket), custom_call_target="tpu_custom_call" | custom-call | flops 131072 | bytes 2048 | tf_op jit(solution)/shard_map/pallas_call | solution.py:289
  (4 shorter events, 0.1 us)
Async XLA Ops:
  0.6 5.0 %copy-start = (bf16[1,1024,1024]{2,1,0:T(8,128)(2,1)S(1)}, bf16[1,1024,1024]{2,1,0:T(8,128)(2,1)}, u32[]{:S(2)}) copy-start(bf16[1,1024,1024]{2,1,0:T(8,128)(2,1)} %matrix.9) | copy-start | bytes 6291460
  0.6 5.8 %copy-start.1 = (bf16[2,128,1024]{2,1,0:T(8,128)(2,1)S(1)}, bf16[2,128,1024]{2,1,0:T(8,128)(2,1)}, u32[]{:S(2)}) copy-start(bf16[2,128,1024]{2,1,0:T(8,128)(2,1)} %stem.3) | copy-start | bytes 1572868
  4.3 7.8 %collective-permute-start = (bf16[128,1024]{1,0:T(8,128)(2,1)S(1)}, bf16[128,1024]{1,0:T(8,128)(2,1)S(1)}, u32[]{:S(2)}, u32[]{:S(2)}) collective-permute-start(bf16[128,1024]{1,0:T(8,128)(2,1)S(1)} %get-tuple-element.23), channel_id=1, source_target_pairs={{128,0},{256,128},{384,256},{129,1},{257,129},{385,257},{130,2},{2... | collective-permute-start | bytes 786440 | tf_op jit(solution)/shard_map/ppermute | solution.py:195
  6.4 5.6 %copy-start.2 = (bf16[2,128,1024]{2,1,0:T(8,128)(2,1)S(1)}, bf16[2,128,1024]{2,1,0:T(8,128)(2,1)}, u32[]{:S(2)}) copy-start(bf16[2,128,1024]{2,1,0:T(8,128)(2,1)} %top.3) | copy-start | bytes 1572868
  7.2 16.1 %collective-permute-start.2 = (bf16[128,1024]{1,0:T(8,128)(2,1)S(1)}, bf16[128,1024]{1,0:T(8,128)(2,1)S(1)}, u32[]{:S(2)}, u32[]{:S(2)}) collective-permute-start(bf16[128,1024]{1,0:T(8,128)(2,1)S(1)} %shard_map.89), channel_id=1, source_target_pairs={{0,128},{128,256},{256,384},{1,129},{129,257},{257,385},{2,130},{1... | collective-permute-start | bytes 786440 | tf_op jit(solution)/shard_map/ppermute | solution.py:195
  12.3 11.2 %collective-permute-start.1 = (bf16[384,1024]{1,0:T(8,128)(2,1)S(1)}, bf16[384,1024]{1,0:T(8,128)(2,1)S(1)}, u32[]{:S(2)}, u32[]{:S(2)}) collective-permute-start(bf16[384,1024]{1,0:T(8,128)(2,1)S(1)} %get-tuple-element.24.packed), channel_id=1, source_target_pairs={{0,1},{1,0},{2,3},{3,2},{4,5},{5,4},{6,7},{7,6},{8,9},{9,8},{10,11... | collective-permute-start | bytes 2359304 | tf_op jit(solution)/shard_map/ppermute | solution.py:199
  96.9 9.5 %collective-permute-start.3 = (bf16[1024,512]{1,0:T(8,128)(2,1)S(1)}, bf16[1024,512]{1,0:T(8,128)(2,1)S(1)}, u32[]{:S(2)}, u32[]{:S(2)}) collective-permute-start(bf16[1024,512]{1,0:T(8,128)(2,1)S(1)} %bitcast.4), channel_id=1, source_target_pairs={{0,1},{1,0},{2,3},{3,2},{4,5},{5,4},{6,7},{7,6},{8,9},{9,8},{10,11... | collective-permute-start | bytes 3145736 | tf_op jit(solution)/shard_map/ppermute | solution.py:199

commit v5 on v4

--- a/solution.py
+++ b/solution.py
@@ -41,7 +41,7 @@
     return (upstream.astype(F32) + inverse * inner).astype(BF16)
 
 
-def call(kernel, in_specs, out_specs, outs, flops, scratch=()):
+def call(kernel, in_specs, out_specs, outs, flops, scratch=(), aliases=None):
     return pl.pallas_call(
         kernel,
         out_shape=[jax.ShapeDtypeStruct(shape, dtype) for shape, dtype in outs],
@@ -52,6 +52,7 @@
             out_specs=out_specs,
             scratch_shapes=list(scratch),
         ),
+        input_output_aliases=aliases or {},
         compiler_params=pltpu.CompilerParams(vmem_limit_bytes=16 << 20),
         cost_estimate=pl.CostEstimate(flops=flops, bytes_accessed=flops // 64, transcendentals=0),
     )
@@ -168,25 +169,28 @@
     result[...] = fresh(rows, matrix[0])
 
 
-def fresh_second(stem, arriving, matrix, after, result, ticket):
+def fresh_second(stem, arriving, matrix, own, handoff, result, done):
+    copy = pltpu.make_async_copy(own, columns_of(result, own, 0), done.at[0])
+    copy.start()
     rows = jnp.where(lax.axis_index("module") == 0, stem[0], arriving[...])
-    result[0] = fresh(rows, matrix[0])
-    ticket[...] = jnp.zeros(TICKET, F32)
-
-
-def joined(own, other, ticket, result, done):
-    half = own.shape[1]
-    here = lax.axis_index("core")
-    copies = [
-        pltpu.make_async_copy(
-            block, result.at[0, :, pl.ds(pl.multiple_of(core * half, half), half)], done.at[number]
-        )
-        for number, (block, core) in enumerate(((own, here), (other, 1 - here)))
-    ]
-    for copy in copies:
-        copy.start()
-    for copy in copies:
-        copy.wait()
+    handoff[0] = fresh(rows, matrix[0])
+    copy.wait()
+
+
+def block_sum(spread, result):
+    result[...] = jnp.sum(spread[...].astype(F32), axis=0).astype(BF16)
+
+
+def columns_of(result, block, core):
+    half = block.shape[1]
+    place = lax.rem(lax.axis_index("core") + core, 2)
+    return result.at[0, :, pl.ds(pl.multiple_of(place * half, half), half)]
+
+
+def joined(partial, other, result, done):
+    copy = pltpu.make_async_copy(other, columns_of(result, other, 1), done.at[0])
+    copy.start()
+    copy.wait()
 
 
 def shift(block, axis, distance):
@@ -269,7 +273,14 @@
     outer, inner = lax.axis_size("x"), lax.axis_size(REST)
     block, piece = width // outer, width // outer // inner
     spread = exchange(part, "x").reshape(outer, block, half)
-    spread = exchange(jnp.sum(spread.astype(F32), axis=0).astype(BF16), REST)
+    (spread,) = call(
+        block_sum,
+        wholes((outer, block, half)),
+        wholes((block, half)),
+        [((block, half), BF16)],
+        count * width,
+    )(spread)
+    spread = exchange(spread, REST)
     spread = spread.reshape(inner, piece, half).astype(F32)
     grad_scale = float(steps * count * lax.axis_size(DP)) ** (-0.5)
     total = (jnp.sum(spread, axis=0) * grad_scale).astype(BF16)
@@ -279,21 +290,23 @@
     total = exchange(total, "x")
     other = swap(total, "core")
 
-    handoff, ticket = call(
+    handoff, partial = call(
         fresh_second,
         [of_step(1, rows), *wholes(rows, matrix), IN_PLACE],
-        wholes((1, *rows), TICKET),
-        [((1, *rows), BF16), (TICKET, F32)],
+        [whole((1, *rows)), IN_PLACE],
+        [((1, *rows), BF16), (matrix, BF16)],
         one,
-    )(stem_input, arriving, *in_hbm(weight), total)
+        scratch=[pltpu.SemaphoreType.DMA((1,))],
+    )(*in_hbm(stem_input), arriving, weight, total)
     (weight_grad,) = call(
         joined,
-        [IN_PLACE] * 3,
+        [IN_PLACE] * 2,
         [IN_PLACE],
         [(matrix, BF16)],
         count * width,
-        scratch=[pltpu.SemaphoreType.DMA((2,))],
-    )(total, other, ticket)
+        scratch=[pltpu.SemaphoreType.DMA((1,))],
+        aliases={0: 0},
+    )(partial, other)
     return weight_grad, handoff, sent_back
 
 

time: 108 us -> 108 us (level)
    pallas_call x2 -> x3, Pallas kernels: 4.31 us -> 4.23 us  [the longest x1 3.11 us: per_device(): call(fresh_second, [of_step(1, rows), *wholes(rows, matrix), IN_PLACE], [...]
where the time goes in v5:
time: 108 us; the launch traced here: 107 us
  blocking collectives  72.3 us (67%)
  starting transfers between devices  21.8 us (20%)
  Pallas kernels  12 us (11%)
    all_to_all x4, blocking collectives, exchange(): return lax.all_to_all(block, axes, 0, 0, tiled=True)  72.3 us
    ppermute x2, starting transfers between devices, swap(): return lax.ppermute(block, axis, [(0, 1), (1, 0)])  15.8 us
    ppermute x2, starting transfers between devices, shift(): return lax.ppermute(block, axis, route)  5.97 us
    pallas_call x1, Pallas kernels, per_device(): call(first_backward, [IN_PLACE] * 5, wholes(*[rows] * 5), [(rows, BF16)]...  3.64 us
    pallas_call x1, Pallas kernels, per_device(): call(fresh_second, [of_step(1, rows), *wholes(rows, matrix), IN_PLACE], [...  3.11 us
  transfers between devices with their start and end apart: 4, of which 2 were waited for; matrix products, arithmetic and copies ran while one was open for 0% of the time, Pallas kernels for 6%

profile of v5, /device:TPU:1, one launch (start us, length us, event | category | flops | bytes accessed | tf_op | source)
XLA Modules:
  0.0 107.4 jit_solution(16997480968068523234)
XLA Ops:
  0.6 0.0 copy-start
  0.6 0.0 copy-start.1
  0.7 3.6 %shard_map.85 = (bf16[128,1024]{1,0:T(8,128)(2,1)S(1)}, bf16[128,1024]{1,0:T(8,128)(2,1)S(1)}, bf16[128,1024]{1,0:T(8,128)(2,1)S(1)}, bf16[128,1024]{1,0:T(8,128)(2,1)S(1)}, bf16[128,1024]{1,0:T(8,128)(2,1)S(1)}) custom-call(s32[1,2]{1,0:T(1,128)} %slots.1, bf16[1,2,128,1024]{3,2,1,0:T(8,128)(2,1)} %replay.1, bf16[1,1024,1024]{2,1,0:T(8,128)(2,1)} %matrix.9, ...), custom_call_target="tpu_custom_call" | custom-call | flops 536870912 | bytes 8388608 | tf_op jit(solution)/shard_map/pallas_call | solution.py:216
  4.3 1.3 %collective-permute-start.1 = (bf16[128,1024]{1,0:T(8,128)(2,1)S(1)}, bf16[128,1024]{1,0:T(8,128)(2,1)S(1)}, u32[]{:S(2)}, u32[]{:S(2)}) collective-permute-start(bf16[128,1024]{1,0:T(8,128)(2,1)S(1)} %get-tuple-element.24), channel_id=1, source_target_pairs={{128,0},{256,128},{384,256},{129,1},{257,129},{385,257},{130,2},{2... | collective-permute-start | bytes 786440 | tf_op jit(solution)/shard_map/ppermute | solution.py:199
  5.6 0.0 copy-done
  5.6 0.8 shard_map.86
  6.4 0.0 copy-start.2
  6.5 0.0 copy-done.1
  6.5 0.7 shard_map.87
  7.2 4.7 %collective-permute-start = (bf16[128,1024]{1,0:T(8,128)(2,1)S(1)}, bf16[128,1024]{1,0:T(8,128)(2,1)S(1)}, u32[]{:S(2)}, u32[]{:S(2)}) collective-permute-start(bf16[128,1024]{1,0:T(8,128)(2,1)S(1)} %shard_map.87), channel_id=1, source_target_pairs={{0,128},{128,256},{256,384},{1,129},{129,257},{257,385},{2,130},{1... | collective-permute-start | bytes 786440 | tf_op jit(solution)/shard_map/ppermute | solution.py:199
  11.9 0.2 collective-permute-done.1.returning
  12.1 0.0 copy-done.2
  12.1 0.1 shard_map.88
  12.3 9.3 %collective-permute-start.2 = (bf16[384,1024]{1,0:T(8,128)(2,1)S(1)}, bf16[384,1024]{1,0:T(8,128)(2,1)S(1)}, u32[]{:S(2)}, u32[]{:S(2)}) collective-permute-start(bf16[384,1024]{1,0:T(8,128)(2,1)S(1)} %get-tuple-element.25.packed), channel_id=1, source_target_pairs={{0,1},{1,0},{2,3},{3,2},{4,5},{5,4},{6,7},{7,6},{8,9},{9,8},{10,11... | collective-permute-start | bytes 2359304 | tf_op jit(solution)/shard_map/ppermute | solution.py:203
  21.5 1.7 %shard_map.89 = (bf16[1,128,1024]{2,1,0:T(8,128)(2,1)}, f32[8,128]{1,0:T(8,128)S(1)}) custom-call(bf16[128,1024]{1,0:T(8,128)(2,1)S(1)} %get-tuple-element.19.rows1, bf16[128,1024]{1,0:T(8,128)(2,1)S(1)} %get-tuple-element.27.pre_grad, bf16[1,1024,1024]{2,1,0:T(8,128)(2,1)S(1)} %copy-done, bf16[128,1024]{1,0:T(8,128)(2,1)S(1)} %get-tuple-element.28.delayed), custom_call_target="tpu_custom_call" | custom-call | flops 128 | bytes 2 | tf_op jit(solution)/shard_map/pallas_call | solution.py:255
  23.3 0.0 collective-permute-done.after.arriving
  23.3 0.2 collective-permute-done.2.pair
  23.4 0.7 shard_map.91
  24.2 17.3 %all_to_all.32.spread = bf16[4,256,512]{2,1,0:T(8,128)(2,1)S(1)} all-to-all(bf16[4,256,512]{2,1,0:T(8,128)(2,1)S(1)} %bitcast.4), channel_id=1, replica_groups=mesh['module'=4,'x'=4,'y_hi'=2,'z'=8,'core'=2] {'x'}, dimensions={0} | all-to-all | bytes 2097152 | tf_op jit(solution)/shard_map/all_to_all | solution.py:207
  41.4 0.1 shard_map.92
  41.6 23.7 %all_to_all.33 = bf16[16,16,512]{2,1,0:T(8,128)(2,1)S(1)} all-to-all(bf16[16,16,512]{2,1,0:T(8,128)(2,1)S(1)} %bitcast.7), channel_id=1, replica_groups=mesh['module'=4,'x'=4,'y_hi'=2,'z'=8,'core'=2] {'y_hi','z'}, dimensions={0} | all-to-all | bytes 524288 | tf_op jit(solution)/shard_map/all_to_all | solution.py:207
  65.3 17.5 %all_to_all.34 = bf16[16,16,512]{2,1,0:T(8,128)(2,1)S(1)} all-to-all(bf16[16,16,512]{2,1,0:T(8,128)(2,1)S(1)} %broadcast_in_dim.6), channel_id=1, replica_groups=mesh['module'=4,'x'=4,'y_hi'=2,'z'=8,'core'=2] {'y_hi','z'}, dimensions={0} | all-to-all | bytes 524288 | tf_op jit(solution)/shard_map/all_to_all | solution.py:207
  82.9 0.1 broadcast_in_dim.16
  82.9 13.8 %all_to_all.35 = bf16[4,256,512]{2,1,0:T(8,128)(2,1)S(1)} all-to-all(bf16[4,256,512]{2,1,0:T(8,128)(2,1)S(1)} %broadcast_in_dim.16), channel_id=1, replica_groups=mesh['module'=4,'x'=4,'y_hi'=2,'z'=8,'core'=2] {'x'}, dimensions={0} | all-to-all | bytes 2097152 | tf_op jit(solution)/shard_map/all_to_all | solution.py:207
  96.8 6.5 %collective-permute-start.3 = (bf16[1024,512]{1,0:T(8,128)(2,1)S(1)}, bf16[1024,512]{1,0:T(8,128)(2,1)S(1)}, u32[]{:S(2)}, u32[]{:S(2)}) collective-permute-start(bf16[1024,512]{1,0:T(8,128)(2,1)S(1)} %bitcast.5), channel_id=1, source_target_pairs={{0,1},{1,0},{2,3},{3,2},{4,5},{5,4},{6,7},{7,6},{8,9},{9,8},{10,11... | collective-permute-start | bytes 3145736 | tf_op jit(solution)/shard_map/ppermute | solution.py:203
  103.3 3.1 %shard_map.93 = (bf16[1,128,1024]{2,1,0:T(8,128)(2,1)}, bf16[1,1024,1024]{2,1,0:T(8,128)(2,1)}) custom-call(bf16[2,128,1024]{2,1,0:T(8,128)(2,1)} %stem.3, bf16[128,1024]{1,0:T(8,128)(2,1)S(1)} %collective-permute-done.after.arriving, bf16[1,1024,1024]{2,1,0:T(8,128)(2,1)S(1)} %copy-done, bf16[1024,512]{1,0:T(8,128)(2,1)S(1)} %bitcast.6), custom_call_target="tpu_custom_call" | custom-call | flops 268435456 | bytes 4194304 | tf_op jit(solution)/shard_map/pallas_call | solution.py:293
  106.4 0.0 collective-permute-done.3.other
  106.4 1.0 shard_map.94
  (4 shorter events, 0.1 us)
Async XLA Ops:
  0.6 5.0 %copy-start = (bf16[1,1024,1024]{2,1,0:T(8,128)(2,1)S(1)}, bf16[1,1024,1024]{2,1,0:T(8,128)(2,1)}, u32[]{:S(2)}) copy-start(bf16[1,1024,1024]{2,1,0:T(8,128)(2,1)} %matrix.9) | copy-start | bytes 6291460
  0.6 5.8 %copy-start.1 = (bf16[2,128,1024]{2,1,0:T(8,128)(2,1)S(1)}, bf16[2,128,1024]{2,1,0:T(8,128)(2,1)}, u32[]{:S(2)}) copy-start(bf16[2,128,1024]{2,1,0:T(8,128)(2,1)} %stem.3) | copy-start | bytes 1572868
  4.3 7.8 %collective-permute-start.1 = (bf16[128,1024]{1,0:T(8,128)(2,1)S(1)}, bf16[128,1024]{1,0:T(8,128)(2,1)S(1)}, u32[]{:S(2)}, u32[]{:S(2)}) collective-permute-start(bf16[128,1024]{1,0:T(8,128)(2,1)S(1)} %get-tuple-element.24), channel_id=1, source_target_pairs={{128,0},{256,128},{384,256},{129,1},{257,129},{385,257},{130,2},{2... | collective-permute-start | bytes 786440 | tf_op jit(solution)/shard_map/ppermute | solution.py:199
  6.4 5.6 %copy-start.2 = (bf16[2,128,1024]{2,1,0:T(8,128)(2,1)S(1)}, bf16[2,128,1024]{2,1,0:T(8,128)(2,1)}, u32[]{:S(2)}) copy-start(bf16[2,128,1024]{2,1,0:T(8,128)(2,1)} %top.3) | copy-start | bytes 1572868
  7.2 16.1 %collective-permute-start = (bf16[128,1024]{1,0:T(8,128)(2,1)S(1)}, bf16[128,1024]{1,0:T(8,128)(2,1)S(1)}, u32[]{:S(2)}, u32[]{:S(2)}) collective-permute-start(bf16[128,1024]{1,0:T(8,128)(2,1)S(1)} %shard_map.87), channel_id=1, source_target_pairs={{0,128},{128,256},{256,384},{1,129},{129,257},{257,385},{2,130},{1... | collective-permute-start | bytes 786440 | tf_op jit(solution)/shard_map/ppermute | solution.py:199
  12.3 11.2 %collective-permute-start.2 = (bf16[384,1024]{1,0:T(8,128)(2,1)S(1)}, bf16[384,1024]{1,0:T(8,128)(2,1)S(1)}, u32[]{:S(2)}, u32[]{:S(2)}) collective-permute-start(bf16[384,1024]{1,0:T(8,128)(2,1)S(1)} %get-tuple-element.25.packed), channel_id=1, source_target_pairs={{0,1},{1,0},{2,3},{3,2},{4,5},{5,4},{6,7},{7,6},{8,9},{9,8},{10,11... | collective-permute-start | bytes 2359304 | tf_op jit(solution)/shard_map/ppermute | solution.py:203
  96.8 9.7 %collective-permute-start.3 = (bf16[1024,512]{1,0:T(8,128)(2,1)S(1)}, bf16[1024,512]{1,0:T(8,128)(2,1)S(1)}, u32[]{:S(2)}, u32[]{:S(2)}) collective-permute-start(bf16[1024,512]{1,0:T(8,128)(2,1)S(1)} %bitcast.5), channel_id=1, source_target_pairs={{0,1},{1,0},{2,3},{3,2},{4,5},{5,4},{6,7},{7,6},{8,9},{9,8},{10,11... | collective-permute-start | bytes 3145736 | tf_op jit(solution)/shard_map/ppermute | solution.py:203

commit v6 on v5

--- a/solution.py
+++ b/solution.py
@@ -270,7 +270,7 @@
         2 * one,
     )(packed, kept, pair, ticket)
 
-    outer, inner = lax.axis_size("x"), lax.axis_size(REST)
+    outer, inner = lax.axis_size("x"), lax.axis_size("z")
     block, piece = width // outer, width // outer // inner
     spread = exchange(part, "x").reshape(outer, block, half)
     (spread,) = call(
@@ -280,12 +280,13 @@
         [((block, half), BF16)],
         count * width,
     )(spread)
-    spread = exchange(spread, REST)
+    spread = exchange(spread, "z")
     spread = spread.reshape(inner, piece, half).astype(F32)
     grad_scale = float(steps * count * lax.axis_size(DP)) ** (-0.5)
-    total = (jnp.sum(spread, axis=0) * grad_scale).astype(BF16)
+    own = jnp.sum(spread, axis=0)
+    total = ((own + swap(own, "y_hi")) * grad_scale).astype(BF16)
     total = jnp.broadcast_to(total[None], (inner, piece, half)).reshape(block, half)
-    total = exchange(total, REST)
+    total = exchange(total, "z")
     total = jnp.broadcast_to(total[None], (outer, block, half)).reshape(width, half)
     total = exchange(total, "x")
     other = swap(total, "core")

time: 108 us -> 105 us (0.972)
  blocking collectives: 72.3 us -> 57.3 us
  starting transfers between devices: 21.8 us -> 31.8 us
  waiting for transfers between devices: 0.4 us -> 2.11 us
    all_to_all x4, blocking collectives: 72.3 us -> 57.3 us  [exchange(): return lax.all_to_all(block, axes, 0, 0, tiled=True)]
    ppermute x2 -> x3, starting transfers between devices: 15.8 us -> 25.8 us  [swap(): return lax.ppermute(block, axis, [(0, 1), (1, 0)])]
    ppermute x2 -> x3, waiting for transfers between devices: 0.16 us -> 1.87 us  [swap(): return lax.ppermute(block, axis, [(0, 1), (1, 0)])]
  transfers between devices with their start and end apart: 4 -> 5, of which waited for: 2 -> 3; matrix products, arithmetic and copies ran while one was open for 0% -> 0% of each run, Pallas kernels for 6% -> 6%
where the time goes in v6:
time: 105 us; the launch traced here: 104 us
  blocking collectives  57.3 us (55%)
  starting transfers between devices  31.8 us (30%)
  Pallas kernels  12 us (11%)
  waiting for transfers between devices  2.11 us (2%)
    all_to_all x4, blocking collectives, exchange(): return lax.all_to_all(block, axes, 0, 0, tiled=True)  57.3 us
    ppermute x3, starting transfers between devices, swap(): return lax.ppermute(block, axis, [(0, 1), (1, 0)])  25.8 us
    ppermute x2, starting transfers between devices, shift(): return lax.ppermute(block, axis, route)  5.97 us
    pallas_call x1, Pallas kernels, per_device(): call(first_backward, [IN_PLACE] * 5, wholes(*[rows] * 5), [(rows, BF16)]...  3.64 us
    pallas_call x1, Pallas kernels, per_device(): call(fresh_second, [of_step(1, rows), *wholes(rows, matrix), IN_PLACE], [...  3.1 us
  transfers between devices with their start and end apart: 5, of which 3 were waited for; matrix products, arithmetic and copies ran while one was open for 0% of the time, Pallas kernels for 6%

profile of v6, /device:TPU:1, one launch (start us, length us, event | category | flops | bytes accessed | tf_op | source)
XLA Modules:
  0.0 104.2 jit_solution(9882991752902009522)
XLA Ops:
  0.6 0.0 copy-start
  0.6 0.0 copy-start.1
  0.7 3.6 %shard_map.85 = (bf16[128,1024]{1,0:T(8,128)(2,1)S(1)}, bf16[128,1024]{1,0:T(8,128)(2,1)S(1)}, bf16[128,1024]{1,0:T(8,128)(2,1)S(1)}, bf16[128,1024]{1,0:T(8,128)(2,1)S(1)}, bf16[128,1024]{1,0:T(8,128)(2,1)S(1)}) custom-call(s32[1,2]{1,0:T(1,128)} %slots.1, bf16[1,2,128,1024]{3,2,1,0:T(8,128)(2,1)} %replay.1, bf16[1,1024,1024]{2,1,0:T(8,128)(2,1)} %matrix.9, ...), custom_call_target="tpu_custom_call" | custom-call | flops 536870912 | bytes 8388608 | tf_op jit(solution)/shard_map/pallas_call | solution.py:216
  4.3 1.3 %collective-permute-start.1 = (bf16[128,1024]{1,0:T(8,128)(2,1)S(1)}, bf16[128,1024]{1,0:T(8,128)(2,1)S(1)}, u32[]{:S(2)}, u32[]{:S(2)}) collective-permute-start(bf16[128,1024]{1,0:T(8,128)(2,1)S(1)} %get-tuple-element.24), channel_id=1, source_target_pairs={{128,0},{256,128},{384,256},{129,1},{257,129},{385,257},{130,2},{2... | collective-permute-start | bytes 786440 | tf_op jit(solution)/shard_map/ppermute | solution.py:199
  5.6 0.0 copy-done
  5.6 0.8 shard_map.86
  6.4 0.0 copy-start.2
  6.5 0.0 copy-done.1
  6.5 0.7 shard_map.87
  7.2 4.7 %collective-permute-start = (bf16[128,1024]{1,0:T(8,128)(2,1)S(1)}, bf16[128,1024]{1,0:T(8,128)(2,1)S(1)}, u32[]{:S(2)}, u32[]{:S(2)}) collective-permute-start(bf16[128,1024]{1,0:T(8,128)(2,1)S(1)} %shard_map.87), channel_id=1, source_target_pairs={{0,128},{128,256},{256,384},{1,129},{129,257},{257,385},{2,130},{1... | collective-permute-start | bytes 786440 | tf_op jit(solution)/shard_map/ppermute | solution.py:199
  11.9 0.2 collective-permute-done.1.returning
  12.1 0.0 copy-done.2
  12.1 0.1 shard_map.88
  12.3 9.3 %collective-permute-start.2 = (bf16[384,1024]{1,0:T(8,128)(2,1)S(1)}, bf16[384,1024]{1,0:T(8,128)(2,1)S(1)}, u32[]{:S(2)}, u32[]{:S(2)}) collective-permute-start(bf16[384,1024]{1,0:T(8,128)(2,1)S(1)} %get-tuple-element.25.packed), channel_id=1, source_target_pairs={{0,1},{1,0},{2,3},{3,2},{4,5},{5,4},{6,7},{7,6},{8,9},{9,8},{10,11... | collective-permute-start | bytes 2359304 | tf_op jit(solution)/shard_map/ppermute | solution.py:203
  21.5 1.7 %shard_map.89 = (bf16[1,128,1024]{2,1,0:T(8,128)(2,1)}, f32[8,128]{1,0:T(8,128)S(1)}) custom-call(bf16[128,1024]{1,0:T(8,128)(2,1)S(1)} %get-tuple-element.19.rows1, bf16[128,1024]{1,0:T(8,128)(2,1)S(1)} %get-tuple-element.27.pre_grad, bf16[1,1024,1024]{2,1,0:T(8,128)(2,1)S(1)} %copy-done, bf16[128,1024]{1,0:T(8,128)(2,1)S(1)} %get-tuple-element.28.delayed), custom_call_target="tpu_custom_call" | custom-call | flops 128 | bytes 2 | tf_op jit(solution)/shard_map/pallas_call | solution.py:255
  23.3 0.0 collective-permute-done.after.arriving
  23.3 0.2 collective-permute-done.2.pair
  23.4 0.7 shard_map.91
  24.2 17.3 %all_to_all.32.spread = bf16[4,256,512]{2,1,0:T(8,128)(2,1)S(1)} all-to-all(bf16[4,256,512]{2,1,0:T(8,128)(2,1)S(1)} %bitcast.4), channel_id=1, replica_groups=mesh['module'=4,'x'=4,'y_hi'=2,'z'=8,'core'=2] {'x'}, dimensions={0} | all-to-all | bytes 2097152 | tf_op jit(solution)/shard_map/all_to_all | solution.py:207
  41.4 0.1 shard_map.92
  41.6 16.1 %all_to_all.33 = bf16[8,32,512]{2,1,0:T(8,128)(2,1)S(1)} all-to-all(bf16[8,32,512]{2,1,0:T(8,128)(2,1)S(1)} %bitcast.7), channel_id=1, replica_groups=mesh['module'=4,'x'=4,'y_hi'=2,'z'=8,'core'=2] {'z'}, dimensions={0} | all-to-all | bytes 524288 | tf_op jit(solution)/shard_map/all_to_all | solution.py:207
  57.7 7.5 %collective-permute-start.3 = (f32[32,512]{1,0:T(8,128)S(1)}, f32[32,512]{1,0:T(8,128)S(1)}, u32[]{:S(2)}, u32[]{:S(2)}) collective-permute-start(f32[32,512]{1,0:T(8,128)S(1)} %convert_reduce_fusion), channel_id=1, source_target_pairs={{0,16},{16,0},{1,17},{17,1},{2,18},{18,2},{3,19},{19,3},{4,20},{20... | collective-permute-start | bytes 196616 | tf_op jit(solution)/shard_map/ppermute | solution.py:203
  65.2 1.7 %collective-permute-done.3 = f32[32,512]{1,0:T(8,128)S(1)} collective-permute-done((f32[32,512]{1,0:T(8,128)S(1)}, f32[32,512]{1,0:T(8,128)S(1)}, u32[]{:S(2)}, u32[]{:S(2)}) %collective-permute-start.3) | collective-permute-done | bytes 65568 | tf_op jit(solution)/shard_map/ppermute | solution.py:203
  67.0 11.7 %all_to_all.34 = bf16[8,32,512]{2,1,0:T(8,128)(2,1)S(1)} all-to-all(bf16[8,32,512]{2,1,0:T(8,128)(2,1)S(1)} %broadcast_in_dim.6), channel_id=1, replica_groups=mesh['module'=4,'x'=4,'y_hi'=2,'z'=8,'core'=2] {'z'}, dimensions={0} | all-to-all | bytes 524288 | tf_op jit(solution)/shard_map/all_to_all | solution.py:207
  78.7 0.1 broadcast_in_dim.16
  78.8 12.2 %all_to_all.35 = bf16[4,256,512]{2,1,0:T(8,128)(2,1)S(1)} all-to-all(bf16[4,256,512]{2,1,0:T(8,128)(2,1)S(1)} %broadcast_in_dim.16), channel_id=1, replica_groups=mesh['module'=4,'x'=4,'y_hi'=2,'z'=8,'core'=2] {'x'}, dimensions={0} | all-to-all | bytes 2097152 | tf_op jit(solution)/shard_map/all_to_all | solution.py:207
  91.0 9.1 %collective-permute-start.4 = (bf16[1024,512]{1,0:T(8,128)(2,1)S(1)}, bf16[1024,512]{1,0:T(8,128)(2,1)S(1)}, u32[]{:S(2)}, u32[]{:S(2)}) collective-permute-start(bf16[1024,512]{1,0:T(8,128)(2,1)S(1)} %bitcast.5), channel_id=1, source_target_pairs={{0,1},{1,0},{2,3},{3,2},{4,5},{5,4},{6,7},{7,6},{8,9},{9,8},{10,11... | collective-permute-start | bytes 3145736 | tf_op jit(solution)/shard_map/ppermute | solution.py:203
  100.1 3.1 %shard_map.93 = (bf16[1,128,1024]{2,1,0:T(8,128)(2,1)}, bf16[1,1024,1024]{2,1,0:T(8,128)(2,1)}) custom-call(bf16[2,128,1024]{2,1,0:T(8,128)(2,1)} %stem.3, bf16[128,1024]{1,0:T(8,128)(2,1)S(1)} %collective-permute-done.after.arriving, bf16[1,1024,1024]{2,1,0:T(8,128)(2,1)S(1)} %copy-done, bf16[1024,512]{1,0:T(8,128)(2,1)S(1)} %bitcast.6), custom_call_target="tpu_custom_call" | custom-call | flops 268435456 | bytes 4194304 | tf_op jit(solution)/shard_map/pallas_call | solution.py:294
  103.2 0.0 collective-permute-done.4.other
  103.2 1.0 shard_map.94
  (4 shorter events, 0.1 us)
Async XLA Ops:
  0.6 5.0 %copy-start = (bf16[1,1024,1024]{2,1,0:T(8,128)(2,1)S(1)}, bf16[1,1024,1024]{2,1,0:T(8,128)(2,1)}, u32[]{:S(2)}) copy-start(bf16[1,1024,1024]{2,1,0:T(8,128)(2,1)} %matrix.9) | copy-start | bytes 6291460
  0.6 5.8 %copy-start.1 = (bf16[2,128,1024]{2,1,0:T(8,128)(2,1)S(1)}, bf16[2,128,1024]{2,1,0:T(8,128)(2,1)}, u32[]{:S(2)}) copy-start(bf16[2,128,1024]{2,1,0:T(8,128)(2,1)} %stem.3) | copy-start | bytes 1572868
  4.3 7.8 %collective-permute-start.1 = (bf16[128,1024]{1,0:T(8,128)(2,1)S(1)}, bf16[128,1024]{1,0:T(8,128)(2,1)S(1)}, u32[]{:S(2)}, u32[]{:S(2)}) collective-permute-start(bf16[128,1024]{1,0:T(8,128)(2,1)S(1)} %get-tuple-element.24), channel_id=1, source_target_pairs={{128,0},{256,128},{384,256},{129,1},{257,129},{385,257},{130,2},{2... | collective-permute-start | bytes 786440 | tf_op jit(solution)/shard_map/ppermute | solution.py:199
  6.4 5.6 %copy-start.2 = (bf16[2,128,1024]{2,1,0:T(8,128)(2,1)S(1)}, bf16[2,128,1024]{2,1,0:T(8,128)(2,1)}, u32[]{:S(2)}) copy-start(bf16[2,128,1024]{2,1,0:T(8,128)(2,1)} %top.3) | copy-start | bytes 1572868
  7.2 16.1 %collective-permute-start = (bf16[128,1024]{1,0:T(8,128)(2,1)S(1)}, bf16[128,1024]{1,0:T(8,128)(2,1)S(1)}, u32[]{:S(2)}, u32[]{:S(2)}) collective-permute-start(bf16[128,1024]{1,0:T(8,128)(2,1)S(1)} %shard_map.87), channel_id=1, source_target_pairs={{0,128},{128,256},{256,384},{1,129},{129,257},{257,385},{2,130},{1... | collective-permute-start | bytes 786440 | tf_op jit(solution)/shard_map/ppermute | solution.py:199
  12.3 11.2 %collective-permute-start.2 = (bf16[384,1024]{1,0:T(8,128)(2,1)S(1)}, bf16[384,1024]{1,0:T(8,128)(2,1)S(1)}, u32[]{:S(2)}, u32[]{:S(2)}) collective-permute-start(bf16[384,1024]{1,0:T(8,128)(2,1)S(1)} %get-tuple-element.25.packed), channel_id=1, source_target_pairs={{0,1},{1,0},{2,3},{3,2},{4,5},{5,4},{6,7},{7,6},{8,9},{9,8},{10,11... | collective-permute-start | bytes 2359304 | tf_op jit(solution)/shard_map/ppermute | solution.py:203
  57.7 9.2 %collective-permute-start.3 = (f32[32,512]{1,0:T(8,128)S(1)}, f32[32,512]{1,0:T(8,128)S(1)}, u32[]{:S(2)}, u32[]{:S(2)}) collective-permute-start(f32[32,512]{1,0:T(8,128)S(1)} %convert_reduce_fusion), channel_id=1, source_target_pairs={{0,16},{16,0},{1,17},{17,1},{2,18},{18,2},{3,19},{19,3},{4,20},{20... | collective-permute-start | bytes 196616 | tf_op jit(solution)/shard_map/ppermute | solution.py:203
  91.0 12.2 %collective-permute-start.4 = (bf16[1024,512]{1,0:T(8,128)(2,1)S(1)}, bf16[1024,512]{1,0:T(8,128)(2,1)S(1)}, u32[]{:S(2)}, u32[]{:S(2)}) collective-permute-start(bf16[1024,512]{1,0:T(8,128)(2,1)S(1)} %bitcast.5), channel_id=1, source_target_pairs={{0,1},{1,0},{2,3},{3,2},{4,5},{5,4},{6,7},{7,6},{8,9},{9,8},{10,11... | collective-permute-start | bytes 3145736 | tf_op jit(solution)/shard_map/ppermute | solution.py:203

commit v7 on v6

--- a/solution.py
+++ b/solution.py
@@ -1,3 +1,5 @@
+import functools
+
 import jax
 import jax.numpy as jnp
 from jax import lax
@@ -169,11 +171,20 @@
     result[...] = fresh(rows, matrix[0])
 
 
-def fresh_second(stem, arriving, matrix, own, handoff, result, done):
+def fresh_second(stem, arriving, matrix, after, handoff, ticket):
+    rows = jnp.where(lax.axis_index("module") == 0, stem[0], arriving[...])
+    handoff[0] = fresh(rows, matrix[0])
+    ticket[...] = jnp.zeros(TICKET, F32)
+
+
+def scaled_total(scale, own, other, ticket, result):
+    total = ((own[...].astype(F32) + other[...].astype(F32)) * scale).astype(BF16)
+    result[...] = jnp.broadcast_to(total[None], result.shape)
+
+
+def own_half(own, result, done):
     copy = pltpu.make_async_copy(own, columns_of(result, own, 0), done.at[0])
     copy.start()
-    rows = jnp.where(lax.axis_index("module") == 0, stem[0], arriving[...])
-    handoff[0] = fresh(rows, matrix[0])
     copy.wait()
 
 
@@ -283,22 +294,35 @@
     spread = exchange(spread, "z")
     spread = spread.reshape(inner, piece, half).astype(F32)
     grad_scale = float(steps * count * lax.axis_size(DP)) ** (-0.5)
-    own = jnp.sum(spread, axis=0)
-    total = ((own + swap(own, "y_hi")) * grad_scale).astype(BF16)
-    total = jnp.broadcast_to(total[None], (inner, piece, half)).reshape(block, half)
+    own = jnp.sum(spread, axis=0).astype(BF16)
+    handoff, ticket = call(
+        fresh_second,
+        [of_step(1, rows), *wholes(rows, matrix), IN_PLACE],
+        wholes((1, *rows), TICKET),
+        [((1, *rows), BF16), (TICKET, F32)],
+        one,
+    )(*in_hbm(stem_input), arriving, weight, own)
+    (total,) = call(
+        functools.partial(scaled_total, grad_scale),
+        [*wholes((piece, half), (piece, half)), whole(TICKET)],
+        wholes((inner, piece, half)),
+        [((inner, piece, half), BF16)],
+        count * width,
+    )(own, swap(own, "y_hi"), ticket)
+    total = total.reshape(block, half)
     total = exchange(total, "z")
     total = jnp.broadcast_to(total[None], (outer, block, half)).reshape(width, half)
     total = exchange(total, "x")
     other = swap(total, "core")
 
-    handoff, partial = call(
-        fresh_second,
-        [of_step(1, rows), *wholes(rows, matrix), IN_PLACE],
-        [whole((1, *rows)), IN_PLACE],
-        [((1, *rows), BF16), (matrix, BF16)],
-        one,
+    (partial,) = call(
+        own_half,
+        [IN_PLACE],
+        [IN_PLACE],
+        [(matrix, BF16)],
+        count * width,
         scratch=[pltpu.SemaphoreType.DMA((1,))],
-    )(*in_hbm(stem_input), arriving, weight, total)
+    )(total)
     (weight_grad,) = call(
         joined,
         [IN_PLACE] * 2,

time: 105 us -> 104 us (level)
  starting transfers between devices: 31.8 us -> 30.7 us
    ppermute x3, starting transfers between devices: 25.8 us -> 24.7 us  [swap(): return lax.ppermute(block, axis, [(0, 1), (1, 0)])]
    pallas_call x1 -> x3, Pallas kernels: 3.1 us -> 3.36 us  [the longest x1 2.35 us: per_device(): call(fresh_second, [of_step(1, rows), *wholes(rows, matrix), IN_PLACE], w...]
  transfers between devices with their start and end apart: 5 -> 5, of which waited for: 3 -> 3; matrix products, arithmetic and copies ran while one was open for 0% -> 0% of each run, Pallas kernels for 6% -> 7%
where the time goes in v7:
time: 104 us; the launch traced here: 103 us
  blocking collectives  57.7 us (55%)
  starting transfers between devices  30.7 us (30%)
  Pallas kernels  12.3 us (12%)
  waiting for transfers between devices  1.67 us (2%)
    all_to_all x4, blocking collectives, exchange(): return lax.all_to_all(block, axes, 0, 0, tiled=True)  57.7 us
    ppermute x3, starting transfers between devices, swap(): return lax.ppermute(block, axis, [(0, 1), (1, 0)])  24.7 us
    ppermute x2, starting transfers between devices, shift(): return lax.ppermute(block, axis, route)  5.97 us
    pallas_call x1, Pallas kernels, per_device(): call(first_backward, [IN_PLACE] * 5, wholes(*[rows] * 5), [(rows, BF16)]...  3.64 us
    pallas_call x1, Pallas kernels, per_device(): call(fresh_second, [of_step(1, rows), *wholes(rows, matrix), IN_PLACE], w...  2.35 us
  transfers between devices with their start and end apart: 5, of which 3 were waited for; matrix products, arithmetic and copies ran while one was open for 0% of the time, Pallas kernels for 7%

profile of v7, /device:TPU:1, one launch (start us, length us, event | category | flops | bytes accessed | tf_op | source)
XLA Modules:
  0.0 103.2 jit_solution(18191051138754872493)
XLA Ops:
  0.6 0.0 copy-start
  0.6 0.0 copy-start.2
  0.7 3.6 %shard_map.85 = (bf16[128,1024]{1,0:T(8,128)(2,1)S(1)}, bf16[128,1024]{1,0:T(8,128)(2,1)S(1)}, bf16[128,1024]{1,0:T(8,128)(2,1)S(1)}, bf16[128,1024]{1,0:T(8,128)(2,1)S(1)}, bf16[128,1024]{1,0:T(8,128)(2,1)S(1)}) custom-call(s32[1,2]{1,0:T(1,128)} %slots.1, bf16[1,2,128,1024]{3,2,1,0:T(8,128)(2,1)} %replay.1, bf16[1,1024,1024]{2,1,0:T(8,128)(2,1)} %matrix.9, ...), custom_call_target="tpu_custom_call" | custom-call | flops 536870912 | bytes 8388608 | tf_op jit(solution)/shard_map/pallas_call | solution.py:227
  4.3 1.3 %collective-permute-start = (bf16[128,1024]{1,0:T(8,128)(2,1)S(1)}, bf16[128,1024]{1,0:T(8,128)(2,1)S(1)}, u32[]{:S(2)}, u32[]{:S(2)}) collective-permute-start(bf16[128,1024]{1,0:T(8,128)(2,1)S(1)} %get-tuple-element.23), channel_id=1, source_target_pairs={{128,0},{256,128},{384,256},{129,1},{257,129},{385,257},{130,2},{2... | collective-permute-start | bytes 786440 | tf_op jit(solution)/shard_map/ppermute | solution.py:210
  5.6 0.0 copy-done
  5.6 0.8 shard_map.86
  6.4 0.0 copy-start.1
  6.5 0.0 copy-done.2
  6.5 0.7 shard_map.89
  7.2 4.7 %collective-permute-start.2 = (bf16[128,1024]{1,0:T(8,128)(2,1)S(1)}, bf16[128,1024]{1,0:T(8,128)(2,1)S(1)}, u32[]{:S(2)}, u32[]{:S(2)}) collective-permute-start(bf16[128,1024]{1,0:T(8,128)(2,1)S(1)} %shard_map.89), channel_id=1, source_target_pairs={{0,128},{128,256},{256,384},{1,129},{129,257},{257,385},{2,130},{1... | collective-permute-start | bytes 786440 | tf_op jit(solution)/shard_map/ppermute | solution.py:210
  11.9 0.2 collective-permute-done.returning
  12.1 0.0 copy-done.1
  12.1 0.1 shard_map.87
  12.3 9.3 %collective-permute-start.1 = (bf16[384,1024]{1,0:T(8,128)(2,1)S(1)}, bf16[384,1024]{1,0:T(8,128)(2,1)S(1)}, u32[]{:S(2)}, u32[]{:S(2)}) collective-permute-start(bf16[384,1024]{1,0:T(8,128)(2,1)S(1)} %get-tuple-element.24.packed), channel_id=1, source_target_pairs={{0,1},{1,0},{2,3},{3,2},{4,5},{5,4},{6,7},{7,6},{8,9},{9,8},{10,11... | collective-permute-start | bytes 2359304 | tf_op jit(solution)/shard_map/ppermute | solution.py:214
  21.5 1.7 %shard_map.88 = (bf16[1,128,1024]{2,1,0:T(8,128)(2,1)}, f32[8,128]{1,0:T(8,128)S(1)}) custom-call(bf16[128,1024]{1,0:T(8,128)(2,1)S(1)} %get-tuple-element.19.rows1, bf16[128,1024]{1,0:T(8,128)(2,1)S(1)} %get-tuple-element.26.pre_grad, bf16[1,1024,1024]{2,1,0:T(8,128)(2,1)S(1)} %copy-done, bf16[128,1024]{1,0:T(8,128)(2,1)S(1)} %get-tuple-element.27.delayed), custom_call_target="tpu_custom_call" | custom-call | flops 128 | bytes 2 | tf_op jit(solution)/shard_map/pallas_call | solution.py:266
  23.2 0.0 collective-permute-done.2.after.arriving
  23.3 0.2 collective-permute-done.1.pair
  23.4 0.7 shard_map.91
  24.2 17.3 %all_to_all.32.spread = bf16[4,256,512]{2,1,0:T(8,128)(2,1)S(1)} all-to-all(bf16[4,256,512]{2,1,0:T(8,128)(2,1)S(1)} %bitcast.6), channel_id=1, replica_groups=mesh['module'=4,'x'=4,'y_hi'=2,'z'=8,'core'=2] {'x'}, dimensions={0} | all-to-all | bytes 2097152 | tf_op jit(solution)/shard_map/all_to_all | solution.py:218
  41.4 0.1 shard_map.92
  41.6 16.1 %all_to_all.33 = bf16[8,32,512]{2,1,0:T(8,128)(2,1)S(1)} all-to-all(bf16[8,32,512]{2,1,0:T(8,128)(2,1)S(1)} %bitcast.7), channel_id=1, replica_groups=mesh['module'=4,'x'=4,'y_hi'=2,'z'=8,'core'=2] {'z'}, dimensions={0} | all-to-all | bytes 524288 | tf_op jit(solution)/shard_map/all_to_all | solution.py:218
  57.8 7.5 %collective-permute-start.3 = (bf16[32,512]{1,0:T(8,128)(2,1)S(1)}, bf16[32,512]{1,0:T(8,128)(2,1)S(1)}, u32[]{:S(2)}, u32[]{:S(2)}) collective-permute-start(bf16[32,512]{1,0:T(8,128)(2,1)S(1)} %reduce_sum.12.after.own), channel_id=1, source_target_pairs={{0,16},{16,0},{1,17},{17,1},{2,18},{18,2},{3,19},{19,3},{4,20},{20... | collective-permute-start | bytes 98312 | tf_op jit(solution)/shard_map/ppermute | solution.py:214
  65.2 2.3 %shard_map.93 = (bf16[1,128,1024]{2,1,0:T(8,128)(2,1)}, f32[8,128]{1,0:T(8,128)S(1)}) custom-call(bf16[2,128,1024]{2,1,0:T(8,128)(2,1)} %stem.3, bf16[128,1024]{1,0:T(8,128)(2,1)S(1)} %collective-permute-done.2.after.arriving, bf16[1,1024,1024]{2,1,0:T(8,128)(2,1)S(1)} %copy-done, bf16[32,512]{1,0:T(8,128)(2,1)S(1)} %reduce_sum.12.after.own), custom_call_target="tpu_custom_call" | custom-call | flops 268435456 | bytes 4194304 | tf_op jit(solution)/shard_map/pallas_call | solution.py:298
  67.6 0.0 collective-permute-done.3.other
  67.6 11.9 %all_to_all.34 = bf16[8,32,512]{2,1,0:T(8,128)(2,1)S(1)} all-to-all(bf16[8,32,512]{2,1,0:T(8,128)(2,1)S(1)} %shard_map.94), channel_id=1, replica_groups=mesh['module'=4,'x'=4,'y_hi'=2,'z'=8,'core'=2] {'z'}, dimensions={0} | all-to-all | bytes 524288 | tf_op jit(solution)/shard_map/all_to_all | solution.py:218
  79.5 0.1 broadcast_in_dim.9
  79.6 12.4 %all_to_all.35 = bf16[4,256,512]{2,1,0:T(8,128)(2,1)S(1)} all-to-all(bf16[4,256,512]{2,1,0:T(8,128)(2,1)S(1)} %broadcast_in_dim.9), channel_id=1, replica_groups=mesh['module'=4,'x'=4,'y_hi'=2,'z'=8,'core'=2] {'x'}, dimensions={0} | all-to-all | bytes 2097152 | tf_op jit(solution)/shard_map/all_to_all | solution.py:218
  92.0 8.0 %collective-permute-start.4 = (bf16[1024,512]{1,0:T(8,128)(2,1)S(1)}, bf16[1024,512]{1,0:T(8,128)(2,1)S(1)}, u32[]{:S(2)}, u32[]{:S(2)}) collective-permute-start(bf16[1024,512]{1,0:T(8,128)(2,1)S(1)} %bitcast.4), channel_id=1, source_target_pairs={{0,1},{1,0},{2,3},{3,2},{4,5},{5,4},{6,7},{7,6},{8,9},{9,8},{10,11... | collective-permute-start | bytes 3145736 | tf_op jit(solution)/shard_map/ppermute | solution.py:214
  100.0 1.0 shard_map.95.partial
  101.0 1.3 %collective-permute-done.4.other = bf16[1024,512]{1,0:T(8,128)(2,1)S(1)} collective-permute-done((bf16[1024,512]{1,0:T(8,128)(2,1)S(1)}, bf16[1024,512]{1,0:T(8,128)(2,1)S(1)}, u32[]{:S(2)}, u32[]{:S(2)}) %collective-permute-start.4) | collective-permute-done | bytes 1048608 | tf_op jit(solution)/shard_map/ppermute | solution.py:214
  102.2 1.0 shard_map.96
  (3 shorter events, 0.1 us)
Async XLA Ops:
  0.6 5.0 %copy-start = (bf16[1,1024,1024]{2,1,0:T(8,128)(2,1)S(1)}, bf16[1,1024,1024]{2,1,0:T(8,128)(2,1)}, u32[]{:S(2)}) copy-start(bf16[1,1024,1024]{2,1,0:T(8,128)(2,1)} %matrix.9) | copy-start | bytes 6291460
  0.6 5.8 %copy-start.2 = (bf16[2,128,1024]{2,1,0:T(8,128)(2,1)S(1)}, bf16[2,128,1024]{2,1,0:T(8,128)(2,1)}, u32[]{:S(2)}) copy-start(bf16[2,128,1024]{2,1,0:T(8,128)(2,1)} %stem.3) | copy-start | bytes 1572868
  4.3 7.8 %collective-permute-start = (bf16[128,1024]{1,0:T(8,128)(2,1)S(1)}, bf16[128,1024]{1,0:T(8,128)(2,1)S(1)}, u32[]{:S(2)}, u32[]{:S(2)}) collective-permute-start(bf16[128,1024]{1,0:T(8,128)(2,1)S(1)} %get-tuple-element.23), channel_id=1, source_target_pairs={{128,0},{256,128},{384,256},{129,1},{257,129},{385,257},{130,2},{2... | collective-permute-start | bytes 786440 | tf_op jit(solution)/shard_map/ppermute | solution.py:210
  6.4 5.6 %copy-start.1 = (bf16[2,128,1024]{2,1,0:T(8,128)(2,1)S(1)}, bf16[2,128,1024]{2,1,0:T(8,128)(2,1)}, u32[]{:S(2)}) copy-start(bf16[2,128,1024]{2,1,0:T(8,128)(2,1)} %top.3) | copy-start | bytes 1572868
  7.2 16.1 %collective-permute-start.2 = (bf16[128,1024]{1,0:T(8,128)(2,1)S(1)}, bf16[128,1024]{1,0:T(8,128)(2,1)S(1)}, u32[]{:S(2)}, u32[]{:S(2)}) collective-permute-start(bf16[128,1024]{1,0:T(8,128)(2,1)S(1)} %shard_map.89), channel_id=1, source_target_pairs={{0,128},{128,256},{256,384},{1,129},{129,257},{257,385},{2,130},{1... | collective-permute-start | bytes 786440 | tf_op jit(solution)/shard_map/ppermute | solution.py:210
  12.3 11.2 %collective-permute-start.1 = (bf16[384,1024]{1,0:T(8,128)(2,1)S(1)}, bf16[384,1024]{1,0:T(8,128)(2,1)S(1)}, u32[]{:S(2)}, u32[]{:S(2)}) collective-permute-start(bf16[384,1024]{1,0:T(8,128)(2,1)S(1)} %get-tuple-element.24.packed), channel_id=1, source_target_pairs={{0,1},{1,0},{2,3},{3,2},{4,5},{5,4},{6,7},{7,6},{8,9},{9,8},{10,11... | collective-permute-start | bytes 2359304 | tf_op jit(solution)/shard_map/ppermute | solution.py:214
  57.8 9.8 %collective-permute-start.3 = (bf16[32,512]{1,0:T(8,128)(2,1)S(1)}, bf16[32,512]{1,0:T(8,128)(2,1)S(1)}, u32[]{:S(2)}, u32[]{:S(2)}) collective-permute-start(bf16[32,512]{1,0:T(8,128)(2,1)S(1)} %reduce_sum.12.after.own), channel_id=1, source_target_pairs={{0,16},{16,0},{1,17},{17,1},{2,18},{18,2},{3,19},{19,3},{4,20},{20... | collective-permute-start | bytes 98312 | tf_op jit(solution)/shard_map/ppermute | solution.py:214
  92.0 10.3 %collective-permute-start.4 = (bf16[1024,512]{1,0:T(8,128)(2,1)S(1)}, bf16[1024,512]{1,0:T(8,128)(2,1)S(1)}, u32[]{:S(2)}, u32[]{:S(2)}) collective-permute-start(bf16[1024,512]{1,0:T(8,128)(2,1)S(1)} %bitcast.4), channel_id=1, source_target_pairs={{0,1},{1,0},{2,3},{3,2},{4,5},{5,4},{6,7},{7,6},{8,9},{9,8},{10,11... | collective-permute-start | bytes 3145736 | tf_op jit(solution)/shard_map/ppermute | solution.py:214

commit v8 on v7

--- a/solution.py
+++ b/solution.py
@@ -150,11 +150,11 @@
     part[...] = (total + matmul(pair[:count], given, (0, 0))).astype(BF16)
 
 
-def marker(ticket, after, result):
-    result[...] = ticket[...]
-
-
-def returned(rows1, pre_grad, matrix, delayed, result, ticket):
+def marker(after, result):
+    result[...] = jnp.zeros(TICKET, F32)
+
+
+def returned(rows1, pre_grad, matrix, delayed, after, result, ticket):
     normed, inverse = normalize(rows1[...])
     result[0] = input_gradient(pre_grad[...], matrix[0], delayed[...], normed, inverse)
     ticket[...] = jnp.zeros(TICKET, F32)
@@ -177,7 +177,7 @@
     ticket[...] = jnp.zeros(TICKET, F32)
 
 
-def scaled_total(scale, own, other, ticket, result):
+def scaled_total(scale, own, other, ticket0, ticket1, result):
     total = ((own[...].astype(F32) + other[...].astype(F32)) * scale).astype(BF16)
     result[...] = jnp.broadcast_to(total[None], result.shape)
 
@@ -263,16 +263,9 @@
         count * width,
     )(rounded0, rounded1, pre_first, slope, returning, top_grad)
     pair = swap(packed, "core")
-    sent_back, ticket = call(
-        returned,
-        wholes(rows, rows, matrix, rows),
-        wholes((1, *rows), TICKET),
-        [((1, *rows), BF16), (TICKET, F32)],
-        count,
-    )(rows1, pre_second, weight, delayed)
     (ticket,) = call(
-        marker, [whole(TICKET), IN_PLACE], wholes(TICKET), [(TICKET, F32)], 100000000000
-    )(ticket, arriving)
+        marker, [IN_PLACE], wholes(TICKET), [(TICKET, F32)], 100000000000
+    )(arriving)
     (part,) = call(
         weight_half,
         [*wholes(packing, columns, packing), IN_PLACE],
@@ -295,6 +288,13 @@
     spread = spread.reshape(inner, piece, half).astype(F32)
     grad_scale = float(steps * count * lax.axis_size(DP)) ** (-0.5)
     own = jnp.sum(spread, axis=0).astype(BF16)
+    sent_back, ticket0 = call(
+        returned,
+        [*wholes(rows, rows, matrix, rows), IN_PLACE],
+        wholes((1, *rows), TICKET),
+        [((1, *rows), BF16), (TICKET, F32)],
+        one,
+    )(rows1, pre_second, weight, delayed, own)
     handoff, ticket = call(
         fresh_second,
         [of_step(1, rows), *wholes(rows, matrix), IN_PLACE],
@@ -304,11 +304,11 @@
     )(*in_hbm(stem_input), arriving, weight, own)
     (total,) = call(
         functools.partial(scaled_total, grad_scale),
-        [*wholes((piece, half), (piece, half)), whole(TICKET)],
+        [*wholes((piece, half), (piece, half)), *wholes(TICKET, TICKET)],
         wholes((inner, piece, half)),
         [((inner, piece, half), BF16)],
         count * width,
-    )(own, swap(own, "y_hi"), ticket)
+    )(own, swap(own, "y_hi"), ticket0, ticket)
     total = total.reshape(block, half)
     total = exchange(total, "z")
     total = jnp.broadcast_to(total[None], (outer, block, half)).reshape(width, half)

time: 104 us -> 105 us (level)
  waiting for transfers between devices: 1.67 us -> 3.38 us
    ppermute x3, waiting for transfers between devices: 1.43 us -> 3.14 us  [swap(): return lax.ppermute(block, axis, [(0, 1), (1, 0)])]
  transfers between devices with their start and end apart: 5 -> 5, of which waited for: 3 -> 3; matrix products, arithmetic and copies ran while one was open for 0% -> 0% of each run, Pallas kernels for 7% -> 6%
where the time goes in v8:
time: 105 us
  blocking collectives  57.6 us (55%)
  starting transfers between devices  30.7 us (29%)
  Pallas kernels  12.2 us (12%)
  waiting for transfers between devices  3.38 us (3%)
    all_to_all x4, blocking collectives, exchange(): return lax.all_to_all(block, axes, 0, 0, tiled=True)  57.6 us
    ppermute x3, starting transfers between devices, swap(): return lax.ppermute(block, axis, [(0, 1), (1, 0)])  24.7 us
    ppermute x2, starting transfers between devices, shift(): return lax.ppermute(block, axis, route)  5.97 us
    pallas_call x1, Pallas kernels, per_device(): call(first_backward, [IN_PLACE] * 5, wholes(*[rows] * 5), [(rows, BF16)]...  3.64 us
    ppermute x3, waiting for transfers between devices, swap(): return lax.ppermute(block, axis, [(0, 1), (1, 0)])  3.14 us
    pallas_call x1, Pallas kernels, per_device(): call(fresh_second, [of_step(1, rows), *wholes(rows, matrix), IN_PLACE], w...  2.34 us
  transfers between devices with their start and end apart: 5, of which 3 were waited for; matrix products, arithmetic and copies ran while one was open for 0% of the time, Pallas kernels for 6%

profile of v8, /device:TPU:1, one launch (start us, length us, event | category | flops | bytes accessed | tf_op | source)
XLA Modules:
  0.0 104.9 jit_solution(15368097242865697880)
XLA Ops:
  0.6 0.0 copy-start
  0.6 0.0 copy-start.2
  0.7 3.6 %shard_map.85 = (bf16[128,1024]{1,0:T(8,128)(2,1)S(1)}, bf16[128,1024]{1,0:T(8,128)(2,1)S(1)}, bf16[128,1024]{1,0:T(8,128)(2,1)S(1)}, bf16[128,1024]{1,0:T(8,128)(2,1)S(1)}, bf16[128,1024]{1,0:T(8,128)(2,1)S(1)}) custom-call(s32[1,2]{1,0:T(1,128)} %slots.1, bf16[1,2,128,1024]{3,2,1,0:T(8,128)(2,1)} %replay.1, bf16[1,1024,1024]{2,1,0:T(8,128)(2,1)} %matrix.9, ...), custom_call_target="tpu_custom_call" | custom-call | flops 536870912 | bytes 8388608 | tf_op jit(solution)/shard_map/pallas_call | solution.py:227
  4.3 1.3 %collective-permute-start = (bf16[128,1024]{1,0:T(8,128)(2,1)S(1)}, bf16[128,1024]{1,0:T(8,128)(2,1)S(1)}, u32[]{:S(2)}, u32[]{:S(2)}) collective-permute-start(bf16[128,1024]{1,0:T(8,128)(2,1)S(1)} %get-tuple-element.23), channel_id=1, source_target_pairs={{128,0},{256,128},{384,256},{129,1},{257,129},{385,257},{130,2},{2... | collective-permute-start | bytes 786440 | tf_op jit(solution)/shard_map/ppermute | solution.py:210
  5.6 0.0 copy-done
  5.6 0.8 shard_map.86
  6.4 0.0 copy-start.1
  6.5 0.0 copy-done.2
  6.5 0.7 shard_map.88
  7.2 4.7 %collective-permute-start.2 = (bf16[128,1024]{1,0:T(8,128)(2,1)S(1)}, bf16[128,1024]{1,0:T(8,128)(2,1)S(1)}, u32[]{:S(2)}, u32[]{:S(2)}) collective-permute-start(bf16[128,1024]{1,0:T(8,128)(2,1)S(1)} %shard_map.88), channel_id=1, source_target_pairs={{0,128},{128,256},{256,384},{1,129},{129,257},{257,385},{2,130},{1... | collective-permute-start | bytes 786440 | tf_op jit(solution)/shard_map/ppermute | solution.py:210
  11.9 0.2 collective-permute-done.returning
  12.1 0.0 copy-done.1
  12.1 0.1 shard_map.87
  12.3 9.3 %collective-permute-start.1 = (bf16[384,1024]{1,0:T(8,128)(2,1)S(1)}, bf16[384,1024]{1,0:T(8,128)(2,1)S(1)}, u32[]{:S(2)}, u32[]{:S(2)}) collective-permute-start(bf16[384,1024]{1,0:T(8,128)(2,1)S(1)} %get-tuple-element.24.packed), channel_id=1, source_target_pairs={{0,1},{1,0},{2,3},{3,2},{4,5},{5,4},{6,7},{7,6},{8,9},{9,8},{10,11... | collective-permute-start | bytes 2359304 | tf_op jit(solution)/shard_map/ppermute | solution.py:214
  21.5 0.0 collective-permute-done.2.after.arriving
  21.5 1.9 %collective-permute-done.1.pair = bf16[384,1024]{1,0:T(8,128)(2,1)S(1)} collective-permute-done((bf16[384,1024]{1,0:T(8,128)(2,1)S(1)}, bf16[384,1024]{1,0:T(8,128)(2,1)S(1)}, u32[]{:S(2)}, u32[]{:S(2)}) %collective-permute-start.1) | collective-permute-done | bytes 786464 | tf_op jit(solution)/shard_map/ppermute | solution.py:214
  23.4 0.7 shard_map.90
  24.2 17.3 %all_to_all.32.spread = bf16[4,256,512]{2,1,0:T(8,128)(2,1)S(1)} all-to-all(bf16[4,256,512]{2,1,0:T(8,128)(2,1)S(1)} %bitcast.6), channel_id=1, replica_groups=mesh['module'=4,'x'=4,'y_hi'=2,'z'=8,'core'=2] {'x'}, dimensions={0} | all-to-all | bytes 2097152 | tf_op jit(solution)/shard_map/all_to_all | solution.py:218
  41.4 0.1 shard_map.91
  41.6 16.1 %all_to_all.33 = bf16[8,32,512]{2,1,0:T(8,128)(2,1)S(1)} all-to-all(bf16[8,32,512]{2,1,0:T(8,128)(2,1)S(1)} %bitcast.7), channel_id=1, replica_groups=mesh['module'=4,'x'=4,'y_hi'=2,'z'=8,'core'=2] {'z'}, dimensions={0} | all-to-all | bytes 524288 | tf_op jit(solution)/shard_map/all_to_all | solution.py:218
  57.7 7.5 %collective-permute-start.3 = (bf16[32,512]{1,0:T(8,128)(2,1)S(1)}, bf16[32,512]{1,0:T(8,128)(2,1)S(1)}, u32[]{:S(2)}, u32[]{:S(2)}) collective-permute-start(bf16[32,512]{1,0:T(8,128)(2,1)S(1)} %reduce_sum.12.after.own), channel_id=1, source_target_pairs={{0,16},{16,0},{1,17},{17,1},{2,18},{18,2},{3,19},{19,3},{4,20},{20... | collective-permute-start | bytes 98312 | tf_op jit(solution)/shard_map/ppermute | solution.py:214
  65.2 1.7 %shard_map.92 = (bf16[1,128,1024]{2,1,0:T(8,128)(2,1)}, f32[8,128]{1,0:T(8,128)S(1)}) custom-call(bf16[128,1024]{1,0:T(8,128)(2,1)S(1)} %get-tuple-element.19.rows1, bf16[128,1024]{1,0:T(8,128)(2,1)S(1)} %get-tuple-element.27.pre_grad, bf16[1,1024,1024]{2,1,0:T(8,128)(2,1)S(1)} %copy-done, bf16[128,1024]{1,0:T(8,128)(2,1)S(1)} %get-tuple-element.28.delayed, ...), custom_call_target="tpu_custom_call" | custom-call | flops 268435456 | bytes 4194304 | tf_op jit(solution)/shard_map/pallas_call | solution.py:291
  66.9 2.3 %shard_map.93 = (bf16[1,128,1024]{2,1,0:T(8,128)(2,1)}, f32[8,128]{1,0:T(8,128)S(1)}) custom-call(bf16[2,128,1024]{2,1,0:T(8,128)(2,1)} %stem.3, bf16[128,1024]{1,0:T(8,128)(2,1)S(1)} %collective-permute-done.2.after.arriving, bf16[1,1024,1024]{2,1,0:T(8,128)(2,1)S(1)} %copy-done, bf16[32,512]{1,0:T(8,128)(2,1)S(1)} %reduce_sum.12.after.own), custom_call_target="tpu_custom_call" | custom-call | flops 268435456 | bytes 4194304 | tf_op jit(solution)/shard_map/pallas_call | solution.py:298
  69.3 0.0 collective-permute-done.3.other
  69.3 11.9 %all_to_all.34 = bf16[8,32,512]{2,1,0:T(8,128)(2,1)S(1)} all-to-all(bf16[8,32,512]{2,1,0:T(8,128)(2,1)S(1)} %shard_map.94), channel_id=1, replica_groups=mesh['module'=4,'x'=4,'y_hi'=2,'z'=8,'core'=2] {'z'}, dimensions={0} | all-to-all | bytes 524288 | tf_op jit(solution)/shard_map/all_to_all | solution.py:218
  81.2 0.1 broadcast_in_dim.9
  81.3 12.4 %all_to_all.35 = bf16[4,256,512]{2,1,0:T(8,128)(2,1)S(1)} all-to-all(bf16[4,256,512]{2,1,0:T(8,128)(2,1)S(1)} %broadcast_in_dim.9), channel_id=1, replica_groups=mesh['module'=4,'x'=4,'y_hi'=2,'z'=8,'core'=2] {'x'}, dimensions={0} | all-to-all | bytes 2097152 | tf_op jit(solution)/shard_map/all_to_all | solution.py:218
  93.6 8.0 %collective-permute-start.4 = (bf16[1024,512]{1,0:T(8,128)(2,1)S(1)}, bf16[1024,512]{1,0:T(8,128)(2,1)S(1)}, u32[]{:S(2)}, u32[]{:S(2)}) collective-permute-start(bf16[1024,512]{1,0:T(8,128)(2,1)S(1)} %bitcast.4), channel_id=1, source_target_pairs={{0,1},{1,0},{2,3},{3,2},{4,5},{5,4},{6,7},{7,6},{8,9},{9,8},{10,11... | collective-permute-start | bytes 3145736 | tf_op jit(solution)/shard_map/ppermute | solution.py:214
  101.6 1.0 shard_map.95.partial
  102.6 1.3 %collective-permute-done.4.other = bf16[1024,512]{1,0:T(8,128)(2,1)S(1)} collective-permute-done((bf16[1024,512]{1,0:T(8,128)(2,1)S(1)}, bf16[1024,512]{1,0:T(8,128)(2,1)S(1)}, u32[]{:S(2)}, u32[]{:S(2)}) %collective-permute-start.4) | collective-permute-done | bytes 1048608 | tf_op jit(solution)/shard_map/ppermute | solution.py:214
  103.9 1.0 shard_map.96
  (3 shorter events, 0.1 us)
Async XLA Ops:
  0.6 5.0 %copy-start = (bf16[1,1024,1024]{2,1,0:T(8,128)(2,1)S(1)}, bf16[1,1024,1024]{2,1,0:T(8,128)(2,1)}, u32[]{:S(2)}) copy-start(bf16[1,1024,1024]{2,1,0:T(8,128)(2,1)} %matrix.9) | copy-start | bytes 6291460
  0.6 5.8 %copy-start.2 = (bf16[2,128,1024]{2,1,0:T(8,128)(2,1)S(1)}, bf16[2,128,1024]{2,1,0:T(8,128)(2,1)}, u32[]{:S(2)}) copy-start(bf16[2,128,1024]{2,1,0:T(8,128)(2,1)} %stem.3) | copy-start | bytes 1572868
  4.3 7.8 %collective-permute-start = (bf16[128,1024]{1,0:T(8,128)(2,1)S(1)}, bf16[128,1024]{1,0:T(8,128)(2,1)S(1)}, u32[]{:S(2)}, u32[]{:S(2)}) collective-permute-start(bf16[128,1024]{1,0:T(8,128)(2,1)S(1)} %get-tuple-element.23), channel_id=1, source_target_pairs={{128,0},{256,128},{384,256},{129,1},{257,129},{385,257},{130,2},{2... | collective-permute-start | bytes 786440 | tf_op jit(solution)/shard_map/ppermute | solution.py:210
  6.4 5.6 %copy-start.1 = (bf16[2,128,1024]{2,1,0:T(8,128)(2,1)S(1)}, bf16[2,128,1024]{2,1,0:T(8,128)(2,1)}, u32[]{:S(2)}) copy-start(bf16[2,128,1024]{2,1,0:T(8,128)(2,1)} %top.3) | copy-start | bytes 1572868
  7.2 14.4 %collective-permute-start.2 = (bf16[128,1024]{1,0:T(8,128)(2,1)S(1)}, bf16[128,1024]{1,0:T(8,128)(2,1)S(1)}, u32[]{:S(2)}, u32[]{:S(2)}) collective-permute-start(bf16[128,1024]{1,0:T(8,128)(2,1)S(1)} %shard_map.88), channel_id=1, source_target_pairs={{0,128},{128,256},{256,384},{1,129},{129,257},{257,385},{2,130},{1... | collective-permute-start | bytes 786440 | tf_op jit(solution)/shard_map/ppermute | solution.py:210
  12.3 11.2 %collective-permute-start.1 = (bf16[384,1024]{1,0:T(8,128)(2,1)S(1)}, bf16[384,1024]{1,0:T(8,128)(2,1)S(1)}, u32[]{:S(2)}, u32[]{:S(2)}) collective-permute-start(bf16[384,1024]{1,0:T(8,128)(2,1)S(1)} %get-tuple-element.24.packed), channel_id=1, source_target_pairs={{0,1},{1,0},{2,3},{3,2},{4,5},{5,4},{6,7},{7,6},{8,9},{9,8},{10,11... | collective-permute-start | bytes 2359304 | tf_op jit(solution)/shard_map/ppermute | solution.py:214
  57.7 11.5 %collective-permute-start.3 = (bf16[32,512]{1,0:T(8,128)(2,1)S(1)}, bf16[32,512]{1,0:T(8,128)(2,1)S(1)}, u32[]{:S(2)}, u32[]{:S(2)}) collective-permute-start(bf16[32,512]{1,0:T(8,128)(2,1)S(1)} %reduce_sum.12.after.own), channel_id=1, source_target_pairs={{0,16},{16,0},{1,17},{17,1},{2,18},{18,2},{3,19},{19,3},{4,20},{20... | collective-permute-start | bytes 98312 | tf_op jit(solution)/shard_map/ppermute | solution.py:214
  93.6 10.3 %collective-permute-start.4 = (bf16[1024,512]{1,0:T(8,128)(2,1)S(1)}, bf16[1024,512]{1,0:T(8,128)(2,1)S(1)}, u32[]{:S(2)}, u32[]{:S(2)}) collective-permute-start(bf16[1024,512]{1,0:T(8,128)(2,1)S(1)} %bitcast.4), channel_id=1, source_target_pairs={{0,1},{1,0},{2,3},{3,2},{4,5},{5,4},{6,7},{7,6},{8,9},{9,8},{10,11... | collective-permute-start | bytes 3145736 | tf_op jit(solution)/shard_map/ppermute | solution.py:214
